TPU v7x, 256 devices: a whole 4x4x8 slice. The times are simulated.
256 devices in a mesh: ctx: 32 (over z, y), kvg: 8 (over x, core).
Axes of the slice: x: 4, y: 4, z: 8, core: 2. Of those that a mesh axis runs over, the one named last changes fastest.
Arguments:
- queries: bfloat16 [8192, 8192], P('ctx', 'kvg'), may hold values from -160 to 160
- keys: bfloat16 [8192, 1024], P(('ctx', 'kvg')), may hold values from -6 to 6
- values: bfloat16 [8192, 1024], P(('ctx', 'kvg')), may hold values from -6 to 6
- segment_ids: int32 [8192], replicated, may hold values from 0 to 11, never falling along the last dimension, each value on 1 to 2049 neighbouring positions
Outputs:
- attended: bfloat16 [8192, 8192], P('ctx', 'kvg')
Inputs may be any that keep to these rules, and one draw needn't show every extreme that they name: `segment_ids`: prompt numbers never fall along the pack; each prompt has 1 to 2049 tokens, and one has exactly that many.
All inputs are finite; a program needn't handle non-finite values.
Results may differ from a plain program's by a relative error of at most 0.0019.
Values may be sent and summed in bfloat16 or wider, within the bound.
No kernel may reach another device: no remote copies, remote signals or barrier semaphores. Data moves between devices by JAX's collectives and lax.ppermute only.
A program may use at most 64 MiB of HBM per device.

v0:
```python
import jax
import jax.numpy as jnp
from jax import lax
from jax.sharding import PartitionSpec as P

HEAD = 128


def passed_along(block, axis, distance):
    devices = range(lax.axis_size(axis))
    route = [(i - distance, i) for i in devices if i - distance in devices]
    return lax.ppermute(block, axis, route)


def tile_part(query_block, key_block, value_block, segment_ids, query_start, key_start):
    rows = query_block.shape[0]
    heads = key_block.shape[1] // HEAD
    group = query_block.shape[1] // (heads * HEAD)
    offsets = jnp.arange(rows, dtype=jnp.int32)
    query_pos = query_start + offsets
    key_pos = key_start + offsets
    query_segs = lax.dynamic_slice_in_dim(segment_ids, query_start, rows, 0)
    key_segs = lax.dynamic_slice_in_dim(segment_ids, jnp.maximum(key_start, 0), rows, 0)
    allowed = (
        (query_segs[:, None] == key_segs[None, :])
        & (key_pos[None, :] <= query_pos[:, None])
        & (key_pos[None, :] >= 0)
    )
    query_four = query_block.reshape(rows, heads, group, HEAD)
    key_three = key_block.reshape(rows, heads, HEAD)
    value_three = value_block.reshape(rows, heads, HEAD)
    scores = jnp.einsum(
        "qhgd,khd->hgqk", query_four, key_three, preferred_element_type=jnp.float32
    ) * (1.0 / HEAD**0.5)
    masked = jnp.where(allowed[None, None], scores, jnp.float32(-1e30))
    top = jnp.max(masked, axis=-1)
    expo = jnp.where(allowed[None, None], jnp.exp(masked - top[..., None]), jnp.float32(0.0))
    total = jnp.sum(expo, axis=-1)
    weights = expo.astype(jnp.bfloat16)
    mixed = jnp.einsum("hgqk,khd->qhgd", weights, value_three, preferred_element_type=jnp.float32)
    return (
        mixed.reshape(rows, heads * group * HEAD),
        top.reshape(heads * group, rows),
        total.reshape(heads * group, rows),
    )


def guarded(query_block, key_block, value_block, segment_ids, query_start, key_start):
    return tile_part(query_block, key_block, value_block, segment_ids, query_start, key_start)


def far_kv(paired, wanted):
    arrived = {}
    for step in wanted:
        arrived[step] = passed_along(paired, "ctx", step)
    return arrived


def combine(parts):
    best = parts[0][1]
    for member in parts[1:]:
        best = jnp.maximum(best, member[1])
    rows = parts[0][0].shape[0]
    columns = best.shape[0]
    numer = jnp.zeros((rows, columns, HEAD), jnp.float32)
    denom = jnp.zeros((columns, rows), jnp.float32)
    for partial_sum, top, total in parts:
        factor = jnp.where(total > 0, jnp.exp(top - best), jnp.float32(0.0))
        numer = numer + jnp.transpose(factor)[:, :, None] * partial_sum.reshape(rows, columns, HEAD)
        denom = denom + factor * total
    mixed = numer / jnp.transpose(denom)[:, :, None]
    return mixed.reshape(rows, columns * HEAD).astype(jnp.bfloat16)


def on_device(queries, keys, values, segment_ids):
    rows = queries.shape[0]
    blocks = lax.axis_size("ctx")
    reach = blocks // 4
    position = lax.axis_index("ctx")
    own_start = position * rows
    key_own, value_own = (
        lax.all_to_all(keys, "kvg", split_axis=1, concat_axis=0, tiled=True),
        lax.all_to_all(values, "kvg", split_axis=1, concat_axis=0, tiled=True),
    )
    paired = jnp.stack([key_own, value_own])
    parts = [tile_part(queries, key_own, value_own, segment_ids, own_start, own_start)]
    kv_blocks = far_kv(paired, list(range(1, reach + 1)))
    for back in range(1, reach + 1):
        key_start = own_start - back * rows
        parts.append(
            guarded(
                queries, kv_blocks[back][0], kv_blocks[back][1], segment_ids, own_start, key_start
            )
        )
    return combine(parts)


def solution(mesh):
    return jax.shard_map(
        on_device,
        mesh=mesh,
        in_specs=(P("ctx", "kvg"), P(("ctx", "kvg"), None), P(("ctx", "kvg"), None), P()),
        out_specs=P("ctx", "kvg"),
        check_vma=False,
    )
```

profile of v0, /device:TPU:88, one launch (start us, length us, event | category | flops | bytes accessed | tf_op | source)
XLA Modules:
  0.0 139.2 jit_solution(8613224543709210111)
XLA Ops:
  0.0 1.5 %copy_bitcast_fusion.1 = bf16[32,8,128]{2,0,1:T(8,128)(2,1)} fusion(bf16[32,1024]{1,0:T(8,128)(2,1)} %param.5), kind=kLoop, calls=%fused_computation.156 | loop fusion | bytes 131072 | tf_op jit(solution)/shard_map/all_to_all | solution.py:82
  1.5 4.3 %all-to-all-start = ((bf16[32,8,128]{2,0,1:T(8,128)(2,1)}), bf16[32,8,128]{2,0,1:T(8,128)(2,1)S(1)}, u32[]{:S(2)}, u32[]{:S(2)}) async-start(bf16[32,8,128]{2,0,1:T(8,128)(2,1)} %copy_bitcast_fusion.1), calls=%async_computation | async-start | bytes 131072 | tf_op jit(solution)/shard_map/all_to_all | solution.py:82
  6.0 1.5 %copy_bitcast_fusion = bf16[32,8,128]{2,0,1:T(8,128)(2,1)} fusion(bf16[32,1024]{1,0:T(8,128)(2,1)} %param.6), kind=kLoop, calls=%fused_computation.155 | loop fusion | bytes 131072 | tf_op jit(solution)/shard_map/all_to_all | solution.py:83
  9.5 2.0 %all-to-all-done = bf16[32,8,128]{2,0,1:T(8,128)(2,1)S(1)} async-done(((bf16[32,8,128]{2,0,1:T(8,128)(2,1)}), bf16[32,8,128]{2,0,1:T(8,128)(2,1)S(1)}, u32[]{:S(2)}, u32[]{:S(2)}) %all-to-all-start) | async-done | bytes 65568 | tf_op jit(solution)/shard_map/all_to_all | solution.py:82
  11.5 3.4 %all-to-all-start.1 = ((bf16[32,8,128]{2,0,1:T(8,128)(2,1)}), bf16[32,8,128]{2,0,1:T(8,128)(2,1)S(1)}, u32[]{:S(2)}, u32[]{:S(2)}) async-start(bf16[32,8,128]{2,0,1:T(8,128)(2,1)} %copy_bitcast_fusion), calls=%async_computation.1 | async-start | bytes 131072 | tf_op jit(solution)/shard_map/all_to_all | solution.py:83
  15.4 5.0 %all-to-all-done.1 = bf16[32,8,128]{2,0,1:T(8,128)(2,1)S(1)} async-done(((bf16[32,8,128]{2,0,1:T(8,128)(2,1)}), bf16[32,8,128]{2,0,1:T(8,128)(2,1)S(1)}, u32[]{:S(2)}, u32[]{:S(2)}) %all-to-all-start.1) | async-done | bytes 65568 | tf_op jit(solution)/shard_map/all_to_all | solution.py:83
  20.4 6.4 %collective-permute-start.7 = (bf16[2,256,128]{2,1,0:T(8,128)(2,1)S(1)}, bf16[2,256,128]{2,1,0:T(8,128)(2,1)}, u32[]{:S(2)}, u32[]{:S(2)}) collective-permute-start(bf16[2,256,128]{2,1,0:T(8,128)(2,1)S(1)} %pad_maximum_fusion), channel_id=1, source_target_pairs={{0,64},{8,72},{16,80},{24,88},{32,96},{40,104},{48,112},{56,120},{... | collective-permute-start | bytes 393224 | tf_op jit(solution)/shard_map/ppermute | solution.py:12
  26.8 3.6 %collective-permute-start.6 = (bf16[2,256,128]{2,1,0:T(8,128)(2,1)S(1)}, bf16[2,256,128]{2,1,0:T(8,128)(2,1)}, u32[]{:S(2)}, u32[]{:S(2)}) collective-permute-start(bf16[2,256,128]{2,1,0:T(8,128)(2,1)S(1)} %pad_maximum_fusion), channel_id=1, source_target_pairs={{0,56},{8,64},{16,72},{24,80},{32,88},{40,96},{48,104},{56,112},{6... | collective-permute-start | bytes 393224 | tf_op jit(solution)/shard_map/ppermute | solution.py:12
  30.3 2.4 %collective-permute-start.5 = (bf16[2,256,128]{2,1,0:T(8,128)(2,1)S(1)}, bf16[2,256,128]{2,1,0:T(8,128)(2,1)}, u32[]{:S(2)}, u32[]{:S(2)}) collective-permute-start(bf16[2,256,128]{2,1,0:T(8,128)(2,1)S(1)} %pad_maximum_fusion), channel_id=1, source_target_pairs={{0,48},{8,56},{16,64},{24,72},{32,80},{40,88},{48,96},{56,104},{64... | collective-permute-start | bytes 393224 | tf_op jit(solution)/shard_map/ppermute | solution.py:12
  32.8 4.5 %collective-permute-start.4 = (bf16[2,256,128]{2,1,0:T(8,128)(2,1)S(1)}, bf16[2,256,128]{2,1,0:T(8,128)(2,1)}, u32[]{:S(2)}, u32[]{:S(2)}) collective-permute-start(bf16[2,256,128]{2,1,0:T(8,128)(2,1)S(1)} %pad_maximum_fusion), channel_id=1, source_target_pairs={{0,40},{8,48},{16,56},{24,64},{32,72},{40,80},{48,88},{56,96},{64,... | collective-permute-start | bytes 393224 | tf_op jit(solution)/shard_map/ppermute | solution.py:12
  37.3 1.9 %collective-permute-start.2 = (bf16[2,256,128]{2,1,0:T(8,128)(2,1)S(1)}, bf16[2,256,128]{2,1,0:T(8,128)(2,1)}, u32[]{:S(2)}, u32[]{:S(2)}) collective-permute-start(bf16[2,256,128]{2,1,0:T(8,128)(2,1)S(1)} %pad_maximum_fusion), channel_id=1, source_target_pairs={{0,24},{8,32},{16,40},{24,48},{32,56},{40,64},{48,72},{56,80},{64,... | collective-permute-start | bytes 393224 | tf_op jit(solution)/shard_map/ppermute | solution.py:12
  39.7 1.6 %fusion.52 = f32[8,256,128]{1,2,0:T(8,128)} fusion(bf16[256,128,1]{1,0,2:T(8,128)(2,1)S(1)} %bitcast.648, f32[256,256,8]{1,0,2:T(8,128)S(1)} %get-tuple-element.51, f32[8,256]{1,0:T(8,128)S(1)} %get-tuple-element.50, pred[256,256]{0,1:T(8,128)(4,1)S(1)} %get-tuple-element.25), kind=kOutput, calls=%fused_computation.62 | convolution fusion | flops 136839168 | bytes 3284992 | tf_op jit(solution)/shard_map/hgqk,khd->qhgd/dot_general | solution.py:40
  41.9 1.6 %copy.163 = f32[256,1024]{1,0:T(8,128)S(1)} copy(f32[256,1024]{0,1:T(8,128)} %bitcast.643) | data formatting | bytes 2097152 | tf_op jit(solution)/shard_map/reshape;reshape | solution.py:69
  43.5 8.4 %collective-permute-done.2 = bf16[2,256,128]{2,1,0:T(8,128)(2,1)} collective-permute-done((bf16[2,256,128]{2,1,0:T(8,128)(2,1)S(1)}, bf16[2,256,128]{2,1,0:T(8,128)(2,1)}, u32[]{:S(2)}, u32[]{:S(2)}) %collective-permute-start.2) | collective-permute-done | bytes 131104 | tf_op jit(solution)/shard_map/ppermute | solution.py:12
  51.8 3.0 %collective-permute-start.3 = (bf16[2,256,128]{2,1,0:T(8,128)(2,1)S(1)}, bf16[2,256,128]{2,1,0:T(8,128)(2,1)S(1)}, u32[]{:S(2)}, u32[]{:S(2)}) collective-permute-start(bf16[2,256,128]{2,1,0:T(8,128)(2,1)S(1)} %pad_maximum_fusion), channel_id=1, source_target_pairs={{0,32},{8,40},{16,48},{24,56},{32,64},{40,72},{48,80},{56,88},{64,... | collective-permute-start | bytes 393224 | tf_op jit(solution)/shard_map/ppermute | solution.py:12
  54.8 1.3 fusion.3
  56.2 2.6 %fusion.43 = f32[128,8,256]{2,0,1:T(8,128)} fusion(f32[256,256,8]{1,0,2:T(8,128)S(1)} %get-tuple-element.45, f32[8,256]{1,0:T(8,128)S(1)} %get-tuple-element.44, pred[256,256]{0,1:T(8,128)(4,1)S(1)} %get-tuple-element.26, bf16[2,256,128]{2,1,0:T(8,128)(2,1)} %collective-permute-done.2), kind=kOutput, calls=%fused_computation.56 | convolution fusion | flops 136839168 | bytes 3284992 | tf_op jit(solution)/shard_map/hgqk,khd->qhgd/dot_general | solution.py:40
  59.2 4.6 %collective-permute-start.1 = (bf16[2,256,128]{2,1,0:T(8,128)(2,1)S(1)}, bf16[2,256,128]{2,1,0:T(8,128)(2,1)}, u32[]{:S(2)}, u32[]{:S(2)}) collective-permute-start(bf16[2,256,128]{2,1,0:T(8,128)(2,1)S(1)} %pad_maximum_fusion), channel_id=1, source_target_pairs={{0,16},{8,24},{16,32},{24,40},{32,48},{40,56},{48,64},{56,72},{64,... | collective-permute-start | bytes 393224 | tf_op jit(solution)/shard_map/ppermute | solution.py:12
  64.3 1.7 %fusion.40 = f32[128,8,256]{2,0,1:T(8,128)} fusion(f32[256,256,8]{1,0,2:T(8,128)S(1)} %get-tuple-element.43, f32[8,256]{1,0:T(8,128)S(1)} %get-tuple-element.42, pred[256,256]{0,1:T(8,128)(4,1)S(1)} %get-tuple-element.27, bf16[2,256,128]{2,1,0:T(8,128)(2,1)S(1)} %collective-permute-done.3), kind=kOutput, calls=%fused_computation.54 | convolution fusion | flops 136839168 | bytes 3284992 | tf_op jit(solution)/shard_map/hgqk,khd->qhgd/dot_general | solution.py:40
  66.6 6.8 %collective-permute-start = (bf16[2,256,128]{2,1,0:T(8,128)(2,1)S(1)}, bf16[2,256,128]{2,1,0:T(8,128)(2,1)S(1)}, u32[]{:S(2)}, u32[]{:S(2)}) collective-permute-start(bf16[2,256,128]{2,1,0:T(8,128)(2,1)S(1)} %pad_maximum_fusion), channel_id=1, source_target_pairs={{0,8},{8,16},{16,24},{24,32},{32,40},{40,48},{48,56},{56,64},{64,7... | collective-permute-start | bytes 393224 | tf_op jit(solution)/shard_map/ppermute | solution.py:12
  73.4 1.3 fusion.5
  74.7 2.5 %fusion.37 = f32[128,8,256]{2,0,1:T(8,128)} fusion(f32[256,256,8]{1,0,2:T(8,128)S(1)} %get-tuple-element.41, f32[8,256]{1,0:T(8,128)S(1)} %get-tuple-element.40, pred[256,256]{0,1:T(8,128)(4,1)S(1)} %get-tuple-element.28, bf16[2,256,128]{2,1,0:T(8,128)(2,1)} %collective-permute-done.4), kind=kOutput, calls=%fused_computation.52 | convolution fusion | flops 136839168 | bytes 3284992 | tf_op jit(solution)/shard_map/hgqk,khd->qhgd/dot_general | solution.py:40
  77.8 1.3 fusion.6
  79.1 2.5 %fusion.34 = f32[128,8,256]{2,0,1:T(8,128)} fusion(f32[256,256,8]{1,0,2:T(8,128)S(1)} %get-tuple-element.39, f32[8,256]{1,0:T(8,128)S(1)} %get-tuple-element.38, pred[256,256]{0,1:T(8,128)(4,1)S(1)} %get-tuple-element.29, bf16[2,256,128]{2,1,0:T(8,128)(2,1)} %collective-permute-done.5), kind=kOutput, calls=%fused_computation.50 | convolution fusion | flops 136839168 | bytes 3284992 | tf_op jit(solution)/shard_map/hgqk,khd->qhgd/dot_general | solution.py:40
  82.1 1.3 fusion.7
  83.5 2.5 %fusion.31 = f32[128,8,256]{2,0,1:T(8,128)} fusion(f32[256,256,8]{1,0,2:T(8,128)S(1)} %get-tuple-element.37, f32[8,256]{1,0:T(8,128)S(1)} %get-tuple-element.36, pred[256,256]{0,1:T(8,128)(4,1)S(1)} %get-tuple-element.30, bf16[2,256,128]{2,1,0:T(8,128)(2,1)} %collective-permute-done.6), kind=kOutput, calls=%fused_computation.48 | convolution fusion | flops 136839168 | bytes 3284992 | tf_op jit(solution)/shard_map/hgqk,khd->qhgd/dot_general | solution.py:40
  87.0 1.7 %fusion.49 = f32[128,8,256]{2,0,1:T(8,128)} fusion(f32[256,256,8]{1,0,2:T(8,128)S(1)} %get-tuple-element.49, f32[8,256]{1,0:T(8,128)S(1)} %get-tuple-element.48, pred[256,256]{0,1:T(8,128)(4,1)S(1)} %get-tuple-element.31, bf16[2,256,128]{2,1,0:T(8,128)(2,1)S(1)} %collective-permute-done), kind=kOutput, calls=%fused_computation.60 | convolution fusion | flops 136839168 | bytes 3284992 | tf_op jit(solution)/shard_map/hgqk,khd->qhgd/dot_general | solution.py:40
  89.2 1.3 fusion.8
  90.5 2.5 %fusion.28 = f32[128,8,256]{2,0,1:T(8,128)} fusion(f32[256,256,8]{1,0,2:T(8,128)S(1)} %get-tuple-element.35, f32[8,256]{1,0:T(8,128)S(1)} %get-tuple-element.34, pred[256,256]{0,1:T(8,128)(4,1)S(1)} %get-tuple-element.32, bf16[2,256,128]{2,1,0:T(8,128)(2,1)} %collective-permute-done.7), kind=kOutput, calls=%fused_computation.46 | convolution fusion | flops 136839168 | bytes 3284992 | tf_op jit(solution)/shard_map/hgqk,khd->qhgd/dot_general | solution.py:40
  93.6 1.6 %copy.175 = f32[256,1024]{1,0:T(8,128)S(1)} copy(f32[256,1024]{0,1:T(8,128)} %bitcast.636) | data formatting | bytes 2097152 | tf_op jit(solution)/shard_map/reshape;reshape | solution.py:69
  95.1 2.6 %copy.179 = f32[256,1024]{1,0:T(8,128)} copy(f32[256,1024]{0,1:T(8,128)} %bitcast.637) | data formatting | bytes 2097152 | tf_op jit(solution)/shard_map/reshape;reshape | solution.py:69
  97.7 2.6 %copy.183 = f32[256,1024]{1,0:T(8,128)} copy(f32[256,1024]{0,1:T(8,128)} %bitcast.638) | data formatting | bytes 2097152 | tf_op jit(solution)/shard_map/reshape;reshape | solution.py:69
  100.3 2.5 %copy.187 = f32[256,1024]{1,0:T(8,128)} copy(f32[256,1024]{0,1:T(8,128)} %bitcast.639) | data formatting | bytes 2097152 | tf_op jit(solution)/shard_map/reshape;reshape | solution.py:69
  102.8 2.5 %copy.191 = f32[256,1024]{1,0:T(8,128)} copy(f32[256,1024]{0,1:T(8,128)} %bitcast.640) | data formatting | bytes 2097152 | tf_op jit(solution)/shard_map/reshape;reshape | solution.py:69
  105.4 2.5 %copy.167 = f32[256,1024]{1,0:T(8,128)} copy(f32[256,1024]{0,1:T(8,128)} %bitcast.641) | data formatting | bytes 2097152 | tf_op jit(solution)/shard_map/reshape;reshape | solution.py:69
  107.9 2.6 %copy.195 = f32[256,1024]{1,0:T(8,128)} copy(f32[256,1024]{0,1:T(8,128)} %bitcast.642) | data formatting | bytes 2097152 | tf_op jit(solution)/shard_map/reshape;reshape | solution.py:69
  110.5 1.3 fusion.2
  112.3 2.5 %fusion.46 = f32[128,8,256]{2,0,1:T(8,128)} fusion(f32[256,256,8]{1,0,2:T(8,128)S(1)} %get-tuple-element.47, f32[8,256]{1,0:T(8,128)S(1)} %get-tuple-element.46, pred[256,256]{0,1:T(8,128)(4,1)S(1)} %get-tuple-element.33, bf16[2,256,128]{2,1,0:T(8,128)(2,1)} %collective-permute-done.1), kind=kOutput, calls=%fused_computation.58 | convolution fusion | flops 136839168 | bytes 3284992 | tf_op jit(solution)/shard_map/hgqk,khd->qhgd/dot_general | solution.py:40
  114.9 2.6 %copy.171 = f32[256,1024]{1,0:T(8,128)} copy(f32[256,1024]{0,1:T(8,128)} %bitcast.644) | data formatting | bytes 2097152 | tf_op jit(solution)/shard_map/reshape;reshape | solution.py:69
  121.5 1.5 %mul.271 = f32[256,8,128]{2,1,0:T(8,128)S(1)} broadcast(f32[256,8]{1,0:T(8,128)} %copy.192), dimensions={0,1} | broadcast | bytes 1056768 | tf_op jit(solution)/shard_map/mul | solution.py:69
  123.0 1.2 mul.268
  124.9 1.3 mul.259
  126.3 1.3 mul.256
  127.6 1.3 mul.253
  128.9 1.3 mul.250
  130.2 1.4 mul.247
  131.6 1.3 div.11
  133.0 6.2 %fusion.54 = bf16[256,1024]{1,0:T(8,128)(2,1)} fusion(f32[32,8,8,128]{3,2,1,0:T(8,128)} %bitcast.635, f32[256,1024]{1,0:T(8,128)S(1)} %copy-done.6, f32[32,8,8,128]{3,2,1,0:T(8,128)S(1)} %bitcast.626, f32[256,1024]{1,0:T(8,128)S(1)} %copy-done.4, f32[32,8,8,128]{3,2,1,0:T(8,128)S(1)} %bitcast.627, f32[256,1024]{1,0:T(8,128)S(1)} %copy-done.3, ...), kind=kLoop, calls=%fused_computation.64 | loop fusion | flops 4980736 | bytes 20447232 | tf_op jit(solution)/shard_map/convert_element_type | solution.py:72
  (65 shorter events, 13.3 us)
Async XLA Ops:
  0.0 39.2 %copy-start = (bf16[256,1024]{1,0:T(8,128)(2,1)S(1)}, bf16[256,1024]{1,0:T(8,128)(2,1)}, u32[]{:S(2)}) copy-start(bf16[256,1024]{1,0:T(8,128)(2,1)} %param.4) | copy-start | bytes 1572868
  1.5 9.9 %all-to-all-start = ((bf16[32,8,128]{2,0,1:T(8,128)(2,1)}), bf16[32,8,128]{2,0,1:T(8,128)(2,1)S(1)}, u32[]{:S(2)}, u32[]{:S(2)}) async-start(bf16[32,8,128]{2,0,1:T(8,128)(2,1)} %copy_bitcast_fusion.1), calls=%async_computation | async-start | bytes 131072 | tf_op jit(solution)/shard_map/all_to_all | solution.py:82
  11.5 8.9 %all-to-all-start.1 = ((bf16[32,8,128]{2,0,1:T(8,128)(2,1)}), bf16[32,8,128]{2,0,1:T(8,128)(2,1)S(1)}, u32[]{:S(2)}, u32[]{:S(2)}) async-start(bf16[32,8,128]{2,0,1:T(8,128)(2,1)} %copy_bitcast_fusion), calls=%async_computation.1 | async-start | bytes 131072 | tf_op jit(solution)/shard_map/all_to_all | solution.py:83
  20.4 68.8 %collective-permute-start.7 = (bf16[2,256,128]{2,1,0:T(8,128)(2,1)S(1)}, bf16[2,256,128]{2,1,0:T(8,128)(2,1)}, u32[]{:S(2)}, u32[]{:S(2)}) collective-permute-start(bf16[2,256,128]{2,1,0:T(8,128)(2,1)S(1)} %pad_maximum_fusion), channel_id=1, source_target_pairs={{0,64},{8,72},{16,80},{24,88},{32,96},{40,104},{48,112},{56,120},{... | collective-permute-start | bytes 393224 | tf_op jit(solution)/shard_map/ppermute | solution.py:12
  26.8 55.4 %collective-permute-start.6 = (bf16[2,256,128]{2,1,0:T(8,128)(2,1)S(1)}, bf16[2,256,128]{2,1,0:T(8,128)(2,1)}, u32[]{:S(2)}, u32[]{:S(2)}) collective-permute-start(bf16[2,256,128]{2,1,0:T(8,128)(2,1)S(1)} %pad_maximum_fusion), channel_id=1, source_target_pairs={{0,56},{8,64},{16,72},{24,80},{32,88},{40,96},{48,104},{56,112},{6... | collective-permute-start | bytes 393224 | tf_op jit(solution)/shard_map/ppermute | solution.py:12
  30.3 47.4 %collective-permute-start.5 = (bf16[2,256,128]{2,1,0:T(8,128)(2,1)S(1)}, bf16[2,256,128]{2,1,0:T(8,128)(2,1)}, u32[]{:S(2)}, u32[]{:S(2)}) collective-permute-start(bf16[2,256,128]{2,1,0:T(8,128)(2,1)S(1)} %pad_maximum_fusion), channel_id=1, source_target_pairs={{0,48},{8,56},{16,64},{24,72},{32,80},{40,88},{48,96},{56,104},{64... | collective-permute-start | bytes 393224 | tf_op jit(solution)/shard_map/ppermute | solution.py:12
  32.8 33.8 %collective-permute-start.4 = (bf16[2,256,128]{2,1,0:T(8,128)(2,1)S(1)}, bf16[2,256,128]{2,1,0:T(8,128)(2,1)}, u32[]{:S(2)}, u32[]{:S(2)}) collective-permute-start(bf16[2,256,128]{2,1,0:T(8,128)(2,1)S(1)} %pad_maximum_fusion), channel_id=1, source_target_pairs={{0,40},{8,48},{16,56},{24,64},{32,72},{40,80},{48,88},{56,96},{64,... | collective-permute-start | bytes 393224 | tf_op jit(solution)/shard_map/ppermute | solution.py:12
  37.3 14.5 %collective-permute-start.2 = (bf16[2,256,128]{2,1,0:T(8,128)(2,1)S(1)}, bf16[2,256,128]{2,1,0:T(8,128)(2,1)}, u32[]{:S(2)}, u32[]{:S(2)}) collective-permute-start(bf16[2,256,128]{2,1,0:T(8,128)(2,1)S(1)} %pad_maximum_fusion), channel_id=1, source_target_pairs={{0,24},{8,32},{16,40},{24,48},{32,56},{40,64},{48,72},{56,80},{64,... | collective-permute-start | bytes 393224 | tf_op jit(solution)/shard_map/ppermute | solution.py:12
  51.8 7.4 %collective-permute-start.3 = (bf16[2,256,128]{2,1,0:T(8,128)(2,1)S(1)}, bf16[2,256,128]{2,1,0:T(8,128)(2,1)S(1)}, u32[]{:S(2)}, u32[]{:S(2)}) collective-permute-start(bf16[2,256,128]{2,1,0:T(8,128)(2,1)S(1)} %pad_maximum_fusion), channel_id=1, source_target_pairs={{0,32},{8,40},{16,48},{24,56},{32,64},{40,72},{48,80},{56,88},{64,... | collective-permute-start | bytes 393224 | tf_op jit(solution)/shard_map/ppermute | solution.py:12
  59.2 51.2 %collective-permute-start.1 = (bf16[2,256,128]{2,1,0:T(8,128)(2,1)S(1)}, bf16[2,256,128]{2,1,0:T(8,128)(2,1)}, u32[]{:S(2)}, u32[]{:S(2)}) collective-permute-start(bf16[2,256,128]{2,1,0:T(8,128)(2,1)S(1)} %pad_maximum_fusion), channel_id=1, source_target_pairs={{0,16},{8,24},{16,32},{24,40},{32,48},{40,56},{48,64},{56,72},{64,... | collective-permute-start | bytes 393224 | tf_op jit(solution)/shard_map/ppermute | solution.py:12
  66.6 19.9 %collective-permute-start = (bf16[2,256,128]{2,1,0:T(8,128)(2,1)S(1)}, bf16[2,256,128]{2,1,0:T(8,128)(2,1)S(1)}, u32[]{:S(2)}, u32[]{:S(2)}) collective-permute-start(bf16[2,256,128]{2,1,0:T(8,128)(2,1)S(1)} %pad_maximum_fusion), channel_id=1, source_target_pairs={{0,8},{8,16},{16,24},{24,32},{32,40},{40,48},{48,56},{56,64},{64,7... | collective-permute-start | bytes 393224 | tf_op jit(solution)/shard_map/ppermute | solution.py:12
  121.5 2.7 %copy-start.9 = (f32[256,8]{1,0:T(8,128)S(1)}, f32[256,8]{1,0:T(8,128)}, u32[]{:S(2)}) copy-start(f32[256,8]{1,0:T(8,128)} %copy.184) | copy-start | bytes 24580
  124.2 3.4 %copy-start.8 = (f32[256,8]{1,0:T(8,128)S(1)}, f32[256,8]{1,0:T(8,128)}, u32[]{:S(2)}) copy-start(f32[256,8]{1,0:T(8,128)} %copy.168) | copy-start | bytes 24580
  124.6 8.3 %copy-start.7 = (f32[256,1024]{1,0:T(8,128)S(1)}, f32[256,1024]{1,0:T(8,128)}, u32[]{:S(2)}) copy-start(f32[256,1024]{1,0:T(8,128)} %copy.171) | copy-start | bytes 3145732
  124.9 8.0 %copy-start.6 = (f32[256,1024]{1,0:T(8,128)S(1)}, f32[256,1024]{1,0:T(8,128)}, u32[]{:S(2)}) copy-start(f32[256,1024]{1,0:T(8,128)} %copy.195) | copy-start | bytes 3145732
  126.3 6.7 %copy-start.5 = (f32[256,1024]{1,0:T(8,128)S(1)}, f32[256,1024]{1,0:T(8,128)}, u32[]{:S(2)}) copy-start(f32[256,1024]{1,0:T(8,128)} %copy.167) | copy-start | bytes 3145732
  127.6 5.3 %copy-start.1 = (f32[256,1024]{1,0:T(8,128)S(1)}, f32[256,1024]{1,0:T(8,128)}, u32[]{:S(2)}) copy-start(f32[256,1024]{1,0:T(8,128)} %copy.179) | copy-start | bytes 3145732
  127.6 5.3 %copy-start.2 = (f32[256,1024]{1,0:T(8,128)S(1)}, f32[256,1024]{1,0:T(8,128)}, u32[]{:S(2)}) copy-start(f32[256,1024]{1,0:T(8,128)} %copy.183) | copy-start | bytes 3145732
  127.6 5.4 %copy-start.3 = (f32[256,1024]{1,0:T(8,128)S(1)}, f32[256,1024]{1,0:T(8,128)}, u32[]{:S(2)}) copy-start(f32[256,1024]{1,0:T(8,128)} %copy.187) | copy-start | bytes 3145732
  127.6 5.4 %copy-start.4 = (f32[256,1024]{1,0:T(8,128)S(1)}, f32[256,1024]{1,0:T(8,128)}, u32[]{:S(2)}) copy-start(f32[256,1024]{1,0:T(8,128)} %copy.191) | copy-start | bytes 3145732
where the time goes:
time: 141 us; the launch traced here: 139 us
  starting transfers between devices  40.9 us (29%)
  local copies, waits for them, and re-layouts  39.4 us (28%)
  matrix products  29.6 us (21%)
  waiting for transfers between devices  15.4 us (11%)
  other arithmetic  13.5 us (10%)
    ppermute x8, starting transfers between devices, passed_along(): return lax.ppermute(block, axis, route)  33.2 us
    another operation x9, local copies, waits for them, and re-layouts, combine(): partial_sum.reshape(rows, columns, HEAD)  21.1 us
    dot_general x9, matrix products, tile_part(): jnp.einsum('hgqk,khd->qhgd', weights, value_three, preferred_element_type...  20.3 us
    mul x9, local copies, waits for them, and re-layouts, combine(): jnp.transpose(factor)[:, :, None] * partial_sum.reshape(rows, columns, HEAD)  10 us
    dot_general x9, matrix products, tile_part(): jnp.einsum('qhgd,khd->hgqk', query_four, key_three, preferred_element_typ...  9.32 us
    ppermute x8, waiting for transfers between devices, passed_along(): return lax.ppermute(block, axis, route)  8.38 us
    convert_element_type x1, other arithmetic, combine(): return mixed.reshape(rows, columns * HEAD).astype(jnp.bfloat16)  6.19 us
    all_to_all x1, waiting for transfers between devices, on_device(): lax.all_to_all(values, 'kvg', split_axis=1, concat_axis=0, tiled=True)  4.99 us
  transfers between devices with their start and end apart: 10, of which 3 were waited for; matrix products, arithmetic and copies ran while one was open for 38% of the time, Pallas kernels for 0%

commit v1 on v0

v1 whole, which is shorter than its diff:
```python
import functools

import jax
import jax.numpy as jnp
import numpy as np
from jax import lax
from jax.experimental import pallas as pl
from jax.experimental.pallas import tpu as pltpu
from jax.sharding import PartitionSpec as P

HEAD = 128
EXP2_SCALE = float(np.log2(np.e) / np.sqrt(HEAD))
MASKED = -1e30
NT = (((1,), (1,)), ((), ()))
WIDE = 4
VMEM = pl.BlockSpec(memory_space=pltpu.VMEM)
SMEM = pl.BlockSpec(memory_space=pltpu.SMEM)


def pack_kernel(groups, k_ref, v_ref, o_ref):
    for g in range(groups):
        o_ref[g, 0] = k_ref[:, g * HEAD : (g + 1) * HEAD]
        o_ref[g, 1] = v_ref[:, g * HEAD : (g + 1) * HEAD]


def pack(keys, values):
    rows, columns = keys.shape
    groups = columns // HEAD
    return pl.pallas_call(
        functools.partial(pack_kernel, groups),
        in_specs=[VMEM, VMEM],
        out_specs=VMEM,
        out_shape=jax.ShapeDtypeStruct((groups, 2, rows, HEAD), keys.dtype),
    )(keys, values)


def outgoing_kernel(shifts, position_ref, own_ref, near_ref, far_ref, *out_refs):
    y = lax.rem(position_ref[0], WIDE)
    for shift, out in zip(shifts, out_refs):
        out[0] = near_ref[...]
        target = lax.rem(y + shift, WIDE)

        @pl.when(y < target)
        def _():
            out[1] = own_ref[...]

        @pl.when(y > target)
        def _():
            out[1] = far_ref[...]


def outgoing(position, own, near, far, shifts):
    shape = jax.ShapeDtypeStruct((2, *own.shape), own.dtype)
    return pl.pallas_call(
        functools.partial(outgoing_kernel, shifts),
        in_specs=[SMEM, VMEM, VMEM, VMEM],
        out_specs=[VMEM] * len(shifts),
        out_shape=[shape] * len(shifts),
    )(position, own, near, far)


def attend_kernel(plan, per_item, own, has_state, final, *refs):
    refs = list(refs)
    position_ref, q_ref, seg_ref = refs[:3]
    buffers = 1 + max(b for b, _, _ in plan)
    kv_refs = refs[3 : 3 + buffers]
    refs = refs[3 + buffers :]
    if has_state:
        acc_in, stat_in = refs[:2]
        refs = refs[2:]
    if final:
        out_ref = refs[0]
        refs = refs[1:]
    else:
        acc_out, stat_out = refs[:2]
        refs = refs[2:]
    k_s, vt_s, bias_s, s_s, p_s, t_s, acc_s = refs

    rows = q_ref.shape[0]
    heads = q_ref.shape[1] // HEAD
    count = len(plan)
    c = position_ref[0]
    q_seg = seg_ref[pl.ds(c, 1), :]
    first_seg = jnp.min(q_seg)
    start = jnp.sum((seg_ref[...] < first_seg).astype(jnp.int32))
    query_bias = jnp.where(q_seg == first_seg, 0.0, MASKED).astype(jnp.float32)
    for i, (b, slot, block_of) in enumerate(plan):
        src = kv_refs[b] if slot is None else kv_refs[b].at[slot]
        k_s[i * rows : (i + 1) * rows] = src[:, 0].reshape(rows, HEAD)
        vt_s[:, i * rows : (i + 1) * rows] = src[:, 1].reshape(rows, HEAD).T
        if own:
            key_seg = jnp.broadcast_to(q_seg.astype(jnp.float32), (rows, rows)).T
            k_pos = lax.broadcasted_iota(jnp.int32, (rows, rows), 0)
            q_pos = lax.broadcasted_iota(jnp.int32, (rows, rows), 1)
            allowed = (key_seg == q_seg.astype(jnp.float32)) & (k_pos <= q_pos)
            bias_s[...] = jnp.where(allowed, 0.0, MASKED).astype(jnp.float32)
        else:
            k_pos = block_of(c) * rows + lax.broadcasted_iota(jnp.int32, (rows, HEAD), 0)
            bias_s[i * rows : (i + 1) * rows] = jnp.where(k_pos >= start, 0.0, MASKED).astype(
                jnp.float32
            )

    splits = count // per_item
    items = [(h, g) for h in range(heads) for g in range(splits)]

    def score(t):
        h, g = items[t]
        s_s[t % 2] = lax.dot_general(
            k_s[g * per_item * rows : (g + 1) * per_item * rows],
            q_ref[:, h * HEAD : (h + 1) * HEAD],
            NT,
            preferred_element_type=jnp.float32,
        )

    def soften(t):
        _, g = items[t]
        for i in range(per_item):
            x = s_s[t % 2, i * rows : (i + 1) * rows]
            at = (g * per_item + i) * rows
            bias = bias_s[at : at + rows]
            x = x + (bias if own else jnp.concatenate([bias] * (rows // HEAD), 1))
            top = jnp.max(x, 0, keepdims=True)
            expo = jnp.exp2((x - top) * EXP2_SCALE)
            t_s[t % 2, i : i + 1] = top if own else top + query_bias
            t_s[t % 2, 8 + i : 9 + i] = jnp.sum(expo, 0, keepdims=True)
            p_s[t % 2, i * rows : (i + 1) * rows] = expo.astype(jnp.bfloat16)

    def mix(t):
        h, g = items[t]
        tops = [t_s[t % 2, i : i + 1] for i in range(per_item)]
        totals = [t_s[t % 2, 8 + i : 9 + i] for i in range(per_item)]
        best = functools.reduce(jnp.maximum, tops)
        acc = total = None
        if g > 0:
            old = t_s[2 + h % 2, 0:1]
            best = jnp.maximum(best, old)
            f = jnp.exp2((old - best) * EXP2_SCALE)
            acc, total = acc_s[h % 2] * f, t_s[2 + h % 2, 8:9] * f
        elif has_state:
            old = stat_in[h, 0:1]
            best = jnp.maximum(best, old)
            f = jnp.exp2((old - best) * EXP2_SCALE)
            acc, total = acc_in[h] * f, stat_in[h, 1:2] * f
        for i in range(per_item):
            at = (g * per_item + i) * rows
            part = jnp.dot(
                vt_s[:, at : at + rows],
                p_s[t % 2, i * rows : (i + 1) * rows],
                preferred_element_type=jnp.float32,
            )
            f = jnp.exp2((tops[i] - best) * EXP2_SCALE)
            acc = part * f if acc is None else acc + part * f
            total = totals[i] * f if total is None else total + totals[i] * f
        if g < splits - 1:
            acc_s[h % 2] = acc
            t_s[2 + h % 2, 0:1] = best
            t_s[2 + h % 2, 8:9] = total
        elif final:
            out_ref[:, h * HEAD : (h + 1) * HEAD] = (acc / total).T.astype(jnp.bfloat16)
        else:
            acc_out[h] = acc
            stat_out[h, 0:1] = best
            stat_out[h, 1:2] = total

    for t in range(len(items) + 2):
        if t >= 2:
            mix(t - 2)
        if 1 <= t <= len(items):
            soften(t - 1)
        if t < len(items):
            score(t)


def attend(position, queries, segments, buffers, plan, per_item, own=False, state=(), final=False):
    rows, columns = queries.shape
    heads = columns // HEAD
    count = len(plan)
    if final:
        out_shape = jax.ShapeDtypeStruct(queries.shape, queries.dtype)
        out_specs = VMEM
    else:
        out_shape = [
            jax.ShapeDtypeStruct((heads, HEAD, rows), jnp.float32),
            jax.ShapeDtypeStruct((heads, 8, rows), jnp.float32),
        ]
        out_specs = [VMEM, VMEM]
    return pl.pallas_call(
        functools.partial(attend_kernel, plan, per_item, own, bool(state), final),
        in_specs=[SMEM] + [VMEM] * (2 + len(buffers) + len(state)),
        out_specs=out_specs,
        out_shape=out_shape,
        scratch_shapes=[
            pltpu.VMEM((count * rows, HEAD), jnp.bfloat16),
            pltpu.VMEM((HEAD, count * rows), jnp.bfloat16),
            pltpu.VMEM((count * rows, rows if own else HEAD), jnp.float32),
            pltpu.VMEM((2, per_item * rows, rows), jnp.float32),
            pltpu.VMEM((2, per_item * rows, rows), jnp.bfloat16),
            pltpu.VMEM((4, 16, rows), jnp.float32),
            pltpu.VMEM((2, HEAD, rows), jnp.float32),
        ],
        compiler_params=pltpu.CompilerParams(vmem_limit_bytes=24 << 20),
        cost_estimate=pl.CostEstimate(
            flops=4 * heads * rows * rows * HEAD * count,
            bytes_accessed=4 * rows * columns,
            transcendentals=heads * rows * rows * count,
        ),
    )(position, queries, segments, *buffers, *state)


def own_block(c):
    return c


def back_block(distance, c):
    return c - distance


def near_row(shift, c):
    y = lax.rem(c, WIDE)
    source = lax.rem(y - shift + WIDE, WIDE)
    return c - y + source - WIDE


def edge_row(shift, c):
    y = lax.rem(c, WIDE)
    source = lax.rem(y - shift + WIDE, WIDE)
    return c - y + source - jnp.where(source < y, 0, 2 * WIDE)


def on_device(queries, keys, values, segment_ids):
    rows = queries.shape[0]
    blocks = lax.axis_size("ctx")
    position = lax.axis_index("ctx").astype(jnp.int32).reshape(1)
    segments = segment_ids.reshape(blocks, rows)
    own = lax.all_to_all(pack(keys, values), "kvg", split_axis=0, concat_axis=0, tiled=True)

    def back(block, distance):
        return lax.ppermute(block, "ctx", [(i, (i + distance) % blocks) for i in range(blocks)])

    def around(block, shift):
        return lax.ppermute(
            block, "ctx", [(i, i - i % WIDE + (i + shift) % WIDE) for i in range(blocks)]
        )

    near = back(own, WIDE)
    far = back(own, 2 * WIDE)
    state = attend(position, queries, segments, [own], [(0, None, own_block)], 1, own=True)
    shifts = (1, 3, 2)
    arrived = [
        around(block, shift)
        for block, shift in zip(outgoing(position, own, near, far, shifts), shifts)
    ]
    plan = [
        (0, None, functools.partial(back_block, WIDE)),
        (1, None, functools.partial(back_block, 2 * WIDE)),
    ]
    state = attend(position, queries, segments, [near, far], plan, 2, state=state)
    plan = []
    for i, shift in enumerate(shifts):
        plan.append((i, 0, functools.partial(near_row, shift)))
        plan.append((i, 1, functools.partial(edge_row, shift)))
    return attend(position, queries, segments, arrived, plan, 3, state=state, final=True)


def solution(mesh):
    return jax.shard_map(
        on_device,
        mesh=mesh,
        in_specs=(P("ctx", "kvg"), P(("ctx", "kvg"), None), P(("ctx", "kvg"), None), P()),
        out_specs=P("ctx", "kvg"),
        check_vma=False,
    )
```

time: 141 us -> 50.2 us (0.36)
  the two profiles are of different devices: /device:TPU:88 before, /device:TPU:8 now
where the time goes in v1:
time: 50.2 us; the launch traced here: 50 us
  waiting for transfers between devices  14.6 us (29%)
  Pallas kernels  13.8 us (27%)
  blocking collectives  10.4 us (21%)
  starting transfers between devices  9.5 us (19%)
  local copies, waits for them, and re-layouts  1.57 us (3%)
    all_to_all x1, blocking collectives, on_device(): lax.all_to_all(pack(keys, values), 'kvg', split_axis=0, concat_axis=0, ti...  10.4 us
    pallas_call x3, Pallas kernels, attend(): pl.pallas_call(functools.partial(attend_kernel, plan, per_item, own, bool...  10.2 us
    ppermute x2, waiting for transfers between devices, back(): lax.ppermute(block, 'ctx', [(i, (i + distance) % blocks) for i in range(b...  9.08 us
    ppermute x3, waiting for transfers between devices, around(): lax.ppermute(block, 'ctx', [(i, i - i % WIDE + (i + shift) % WIDE) for i...  5.56 us
    ppermute x2, starting transfers between devices, back(): lax.ppermute(block, 'ctx', [(i, (i + distance) % blocks) for i in range(b...  5.19 us
    ppermute x3, starting transfers between devices, around(): lax.ppermute(block, 'ctx', [(i, i - i % WIDE + (i + shift) % WIDE) for i...  4.32 us
    pallas_call x1, Pallas kernels, outgoing(): pl.pallas_call(functools.partial(outgoing_kernel, shifts), in_specs=[SMEM...  1.97 us
    pallas_call x1, Pallas kernels, pack(): pl.pallas_call(functools.partial(pack_kernel, groups), in_specs=[VMEM, VM...  1.61 us
  transfers between devices with their start and end apart: 5, of which 5 were waited for; matrix products, arithmetic and copies ran while one was open for 0% of the time, Pallas kernels for 8%

profile of v1, /device:TPU:8, one launch (start us, length us, event | category | flops | bytes accessed | tf_op | source)
XLA Modules:
  0.0 50.0 jit_solution(4414864536643268048)
XLA Ops:
  0.0 0.0 copy-start.6
  0.0 1.6 %shard_map.46 = bf16[8,2,32,128]{3,2,1,0:T(8,128)(2,1)} custom-call(bf16[32,1024]{1,0:T(8,128)(2,1)} %k_ref.1, bf16[32,1024]{1,0:T(8,128)(2,1)} %v_ref.1), custom_call_target="tpu_custom_call" | custom-call | tf_op jit(solution)/shard_map/pallas_call | solution.py:29
  1.6 10.4 %all_to_all.5.own_ref.refs_3_ = bf16[8,2,32,128]{3,2,1,0:T(8,128)(2,1)S(1)} all-to-all(bf16[8,2,32,128]{3,2,1,0:T(8,128)(2,1)} %shard_map.46), channel_id=1, replica_groups=mesh['ctx'=32,'kvg'=8] {'kvg'}, dimensions={0} | all-to-all | bytes 262144 | tf_op jit(solution)/shard_map/all_to_all | solution.py:235
  12.0 0.0 copy-start
  12.0 1.9 %collective-permute-start = (bf16[8,2,32,128]{3,2,1,0:T(8,128)(2,1)S(1)}, bf16[8,2,32,128]{3,2,1,0:T(8,128)(2,1)S(1)}, u32[]{:S(2)}, u32[]{:S(2)}) collective-permute-start(bf16[8,2,32,128]{3,2,1,0:T(8,128)(2,1)S(1)} %all_to_all.5.own_ref.refs_3_), channel_id=1, source_target_pairs={{0,32},{8,40},{16,48},{24,56},{32,64},{40,72},{48,80},{56,88},{64,... | collective-permute-start | bytes 393224 | tf_op jit(solution)/shard_map/ppermute | solution.py:238
  14.0 3.3 %collective-permute-start.1 = (bf16[8,2,32,128]{3,2,1,0:T(8,128)(2,1)S(1)}, bf16[8,2,32,128]{3,2,1,0:T(8,128)(2,1)S(1)}, u32[]{:S(2)}, u32[]{:S(2)}) collective-permute-start(bf16[8,2,32,128]{3,2,1,0:T(8,128)(2,1)S(1)} %all_to_all.5.own_ref.refs_3_), channel_id=1, source_target_pairs={{0,64},{8,72},{16,80},{24,88},{32,96},{40,104},{48,112},{56,120},{... | collective-permute-start | bytes 393224 | tf_op jit(solution)/shard_map/ppermute | solution.py:238
  17.2 5.8 %collective-permute-done.near_ref.refs_3_ = bf16[8,2,32,128]{3,2,1,0:T(8,128)(2,1)S(1)} collective-permute-done((bf16[8,2,32,128]{3,2,1,0:T(8,128)(2,1)S(1)}, bf16[8,2,32,128]{3,2,1,0:T(8,128)(2,1)S(1)}, u32[]{:S(2)}, u32[]{:S(2)}) %collective-permute-start) | collective-permute-done | bytes 131104 | tf_op jit(solution)/shard_map/ppermute | solution.py:238
  23.0 0.0 copy-start.2
  23.0 3.3 %collective-permute-done.1.far_ref.refs_4_ = bf16[8,2,32,128]{3,2,1,0:T(8,128)(2,1)S(1)} collective-permute-done((bf16[8,2,32,128]{3,2,1,0:T(8,128)(2,1)S(1)}, bf16[8,2,32,128]{3,2,1,0:T(8,128)(2,1)S(1)}, u32[]{:S(2)}, u32[]{:S(2)}) %collective-permute-start.1) | collective-permute-done | bytes 131104 | tf_op jit(solution)/shard_map/ppermute | solution.py:238
  26.3 0.0 copy-start.4
  26.3 0.0 copy-done
  26.3 0.0 copy-done.2
  26.3 0.6 %copy-done.4 = bf16[8,2,32,128]{3,2,1,0:T(8,128)(2,1)} copy-done((bf16[8,2,32,128]{3,2,1,0:T(8,128)(2,1)}, bf16[8,2,32,128]{3,2,1,0:T(8,128)(2,1)S(1)}, u32[]{:S(2)}) %copy-start.4) | copy-done | bytes 131096
  27.0 0.0 copy-start.7
  27.0 2.0 %shard_map.47 = (bf16[2,8,2,32,128]{4,3,2,1,0:T(8,128)(2,1)}, bf16[2,8,2,32,128]{4,3,2,1,0:T(8,128)(2,1)}, bf16[2,8,2,32,128]{4,3,2,1,0:T(8,128)(2,1)}) custom-call(s32[1]{0:T(128)} %bitcast.position_ref.refs_0_, bf16[8,2,32,128]{3,2,1,0:T(8,128)(2,1)} %copy-done, bf16[8,2,32,128]{3,2,1,0:T(8,128)(2,1)} %copy-done.2, bf16[8,2,32,128]{3,2,1,0:T(8,128)(2,1)} %copy-done.4), custom_call_target="tpu_custom_call" | custom-call | tf_op jit(solution)/shard_map/pallas_call | solution.py:54
  28.9 1.6 %collective-permute-start.2 = (bf16[2,8,2,32,128]{4,3,2,1,0:T(8,128)(2,1)}, bf16[2,8,2,32,128]{4,3,2,1,0:T(8,128)(2,1)S(1)}, u32[]{:S(2)}, u32[]{:S(2)}) collective-permute-start(bf16[2,8,2,32,128]{4,3,2,1,0:T(8,128)(2,1)} %get-tuple-element.12), channel_id=1, source_target_pairs={{0,8},{8,16},{16,24},{24,0},{32,40},{40,48},{48,56},{56,32},{64,72... | collective-permute-start | bytes 786440 | tf_op jit(solution)/shard_map/ppermute | solution.py:241
  30.5 0.5 collective-permute-start.3
  31.0 2.3 %collective-permute-start.4 = (bf16[2,8,2,32,128]{4,3,2,1,0:T(8,128)(2,1)}, bf16[2,8,2,32,128]{4,3,2,1,0:T(8,128)(2,1)S(1)}, u32[]{:S(2)}, u32[]{:S(2)}) collective-permute-start(bf16[2,8,2,32,128]{4,3,2,1,0:T(8,128)(2,1)} %get-tuple-element.14), channel_id=1, source_target_pairs={{0,16},{8,24},{16,0},{24,8},{32,48},{40,56},{48,32},{56,40},{64,80... | collective-permute-start | bytes 786440 | tf_op jit(solution)/shard_map/ppermute | solution.py:241
  33.2 0.0 copy-done.7
  33.3 0.0 copy-done.6
  33.3 0.0 copy-start.1
  33.3 0.9 %copy-done.1 = bf16[8,2,32,128]{3,2,1,0:T(8,128)(2,1)S(1)} copy-done((bf16[8,2,32,128]{3,2,1,0:T(8,128)(2,1)S(1)}, bf16[8,2,32,128]{3,2,1,0:T(8,128)(2,1)}, u32[]{:S(2)}) %copy-start.1) | copy-done | bytes 131096
  34.2 0.0 copy-start.3
  34.2 0.0 copy-start.5
  34.2 1.5 %shard_map.48 = (f32[8,128,256]{2,1,0:T(8,128)S(1)}, f32[8,8,256]{2,1,0:T(8,128)S(1)}) custom-call(s32[1]{0:T(128)} %bitcast.position_ref.refs_0_, bf16[256,1024]{1,0:T(8,128)(2,1)S(1)} %copy-done.6, s32[32,256]{1,0:T(8,128)S(1)} %reshape.7.refs_2_, bf16[8,2,32,128]{3,2,1,0:T(8,128)(2,1)S(1)} %copy-done.1), custom_call_target="tpu_custom_call" | custom-call | flops 268435456 | bytes 1048576 | tf_op jit(solution)/shard_map/pallas_call | solution.py:187
  35.7 0.0 copy-done.3
  35.7 0.0 copy-done.5
  35.7 2.3 %shard_map.49 = (f32[8,128,256]{2,1,0:T(8,128)S(1)}, f32[8,8,256]{2,1,0:T(8,128)S(1)}) custom-call(s32[1]{0:T(128)} %bitcast.position_ref.refs_0_, bf16[256,1024]{1,0:T(8,128)(2,1)S(1)} %copy-done.6, s32[32,256]{1,0:T(8,128)S(1)} %reshape.7.refs_2_, bf16[8,2,32,128]{3,2,1,0:T(8,128)(2,1)S(1)} %copy-done.3, bf16[8,2,32,128]{3,2,1,0:T(8,128)(2,1)S(1)} %copy-done.5, ...), custom_call_target="tpu_custom_call" | custom-call | flops 536870912 | bytes 1048576 | tf_op jit(solution)/shard_map/pallas_call | solution.py:187
  38.0 0.4 collective-permute-done.2.refs_3_
  38.4 0.9 %collective-permute-done.3.refs_4_ = bf16[2,8,2,32,128]{4,3,2,1,0:T(8,128)(2,1)S(1)} collective-permute-done((bf16[2,8,2,32,128]{4,3,2,1,0:T(8,128)(2,1)}, bf16[2,8,2,32,128]{4,3,2,1,0:T(8,128)(2,1)S(1)}, u32[]{:S(2)}, u32[]{:S(2)}) %collective-permute-start.3) | collective-permute-done | bytes 262176 | tf_op jit(solution)/shard_map/ppermute | solution.py:241
  39.2 4.3 %collective-permute-done.4.refs_5_ = bf16[2,8,2,32,128]{4,3,2,1,0:T(8,128)(2,1)S(1)} collective-permute-done((bf16[2,8,2,32,128]{4,3,2,1,0:T(8,128)(2,1)}, bf16[2,8,2,32,128]{4,3,2,1,0:T(8,128)(2,1)S(1)}, u32[]{:S(2)}, u32[]{:S(2)}) %collective-permute-start.4) | collective-permute-done | bytes 262176 | tf_op jit(solution)/shard_map/ppermute | solution.py:241
  43.6 6.4 %shard_map.50 = bf16[256,1024]{1,0:T(8,128)(2,1)} custom-call(s32[1]{0:T(128)} %bitcast.position_ref.refs_0_, bf16[256,1024]{1,0:T(8,128)(2,1)S(1)} %copy-done.6, s32[32,256]{1,0:T(8,128)S(1)} %reshape.7.refs_2_, bf16[2,8,2,32,128]{4,3,2,1,0:T(8,128)(2,1)S(1)} %collective-permute-done.2.refs_3_, ...), custom_call_target="tpu_custom_call" | custom-call | flops 1610612736 | bytes 1048576 | tf_op jit(solution)/shard_map/pallas_call | solution.py:187
  (1 shorter events, 0.0 us)
Async XLA Ops:
  0.0 33.3 %copy-start.6 = (bf16[256,1024]{1,0:T(8,128)(2,1)S(1)}, bf16[256,1024]{1,0:T(8,128)(2,1)}, u32[]{:S(2)}) copy-start(bf16[256,1024]{1,0:T(8,128)(2,1)} %refs_1_.5) | copy-start | bytes 1572868
  12.0 14.3 %copy-start = (bf16[8,2,32,128]{3,2,1,0:T(8,128)(2,1)}, bf16[8,2,32,128]{3,2,1,0:T(8,128)(2,1)S(1)}, u32[]{:S(2)}) copy-start(bf16[8,2,32,128]{3,2,1,0:T(8,128)(2,1)S(1)} %all_to_all.5.own_ref.refs_3_) | copy-start | bytes 393220
  12.0 10.9 %collective-permute-start = (bf16[8,2,32,128]{3,2,1,0:T(8,128)(2,1)S(1)}, bf16[8,2,32,128]{3,2,1,0:T(8,128)(2,1)S(1)}, u32[]{:S(2)}, u32[]{:S(2)}) collective-permute-start(bf16[8,2,32,128]{3,2,1,0:T(8,128)(2,1)S(1)} %all_to_all.5.own_ref.refs_3_), channel_id=1, source_target_pairs={{0,32},{8,40},{16,48},{24,56},{32,64},{40,72},{48,80},{56,88},{64,... | collective-permute-start | bytes 393224 | tf_op jit(solution)/shard_map/ppermute | solution.py:238
  14.0 12.4 %collective-permute-start.1 = (bf16[8,2,32,128]{3,2,1,0:T(8,128)(2,1)S(1)}, bf16[8,2,32,128]{3,2,1,0:T(8,128)(2,1)S(1)}, u32[]{:S(2)}, u32[]{:S(2)}) collective-permute-start(bf16[8,2,32,128]{3,2,1,0:T(8,128)(2,1)S(1)} %all_to_all.5.own_ref.refs_3_), channel_id=1, source_target_pairs={{0,64},{8,72},{16,80},{24,88},{32,96},{40,104},{48,112},{56,120},{... | collective-permute-start | bytes 393224 | tf_op jit(solution)/shard_map/ppermute | solution.py:238
  23.0 3.3 %copy-start.2 = (bf16[8,2,32,128]{3,2,1,0:T(8,128)(2,1)}, bf16[8,2,32,128]{3,2,1,0:T(8,128)(2,1)S(1)}, u32[]{:S(2)}) copy-start(bf16[8,2,32,128]{3,2,1,0:T(8,128)(2,1)S(1)} %collective-permute-done.near_ref.refs_3_) | copy-start | bytes 393220
  26.3 0.6 %copy-start.4 = (bf16[8,2,32,128]{3,2,1,0:T(8,128)(2,1)}, bf16[8,2,32,128]{3,2,1,0:T(8,128)(2,1)S(1)}, u32[]{:S(2)}) copy-start(bf16[8,2,32,128]{3,2,1,0:T(8,128)(2,1)S(1)} %collective-permute-done.1.far_ref.refs_4_) | copy-start | bytes 393220
  27.0 6.3 %copy-start.7 = (s32[8192]{0:T(1024)S(1)}, s32[8192]{0:T(1024)}, u32[]{:S(2)}) copy-start(s32[8192]{0:T(1024)} %param.7) | copy-start | bytes 98308
  28.9 9.5 %collective-permute-start.2 = (bf16[2,8,2,32,128]{4,3,2,1,0:T(8,128)(2,1)}, bf16[2,8,2,32,128]{4,3,2,1,0:T(8,128)(2,1)S(1)}, u32[]{:S(2)}, u32[]{:S(2)}) collective-permute-start(bf16[2,8,2,32,128]{4,3,2,1,0:T(8,128)(2,1)} %get-tuple-element.12), channel_id=1, source_target_pairs={{0,8},{8,16},{16,24},{24,0},{32,40},{40,48},{48,56},{56,32},{64,72... | collective-permute-start | bytes 786440 | tf_op jit(solution)/shard_map/ppermute | solution.py:241
  30.5 8.7 %collective-permute-start.3 = (bf16[2,8,2,32,128]{4,3,2,1,0:T(8,128)(2,1)}, bf16[2,8,2,32,128]{4,3,2,1,0:T(8,128)(2,1)S(1)}, u32[]{:S(2)}, u32[]{:S(2)}) collective-permute-start(bf16[2,8,2,32,128]{4,3,2,1,0:T(8,128)(2,1)} %get-tuple-element.13), channel_id=1, source_target_pairs={{0,24},{8,0},{16,8},{24,16},{32,56},{40,32},{48,40},{56,48},{64,88... | collective-permute-start | bytes 786440 | tf_op jit(solution)/shard_map/ppermute | solution.py:241
  31.0 12.6 %collective-permute-start.4 = (bf16[2,8,2,32,128]{4,3,2,1,0:T(8,128)(2,1)}, bf16[2,8,2,32,128]{4,3,2,1,0:T(8,128)(2,1)S(1)}, u32[]{:S(2)}, u32[]{:S(2)}) collective-permute-start(bf16[2,8,2,32,128]{4,3,2,1,0:T(8,128)(2,1)} %get-tuple-element.14), channel_id=1, source_target_pairs={{0,16},{8,24},{16,0},{24,8},{32,48},{40,56},{48,32},{56,40},{64,80... | collective-permute-start | bytes 786440 | tf_op jit(solution)/shard_map/ppermute | solution.py:241
  33.3 0.9 %copy-start.1 = (bf16[8,2,32,128]{3,2,1,0:T(8,128)(2,1)S(1)}, bf16[8,2,32,128]{3,2,1,0:T(8,128)(2,1)}, u32[]{:S(2)}) copy-start(bf16[8,2,32,128]{3,2,1,0:T(8,128)(2,1)} %copy-done) | copy-start | bytes 393220
  34.2 1.5 %copy-start.3 = (bf16[8,2,32,128]{3,2,1,0:T(8,128)(2,1)S(1)}, bf16[8,2,32,128]{3,2,1,0:T(8,128)(2,1)}, u32[]{:S(2)}) copy-start(bf16[8,2,32,128]{3,2,1,0:T(8,128)(2,1)} %copy-done.2) | copy-start | bytes 393220
  34.2 1.5 %copy-start.5 = (bf16[8,2,32,128]{3,2,1,0:T(8,128)(2,1)S(1)}, bf16[8,2,32,128]{3,2,1,0:T(8,128)(2,1)}, u32[]{:S(2)}) copy-start(bf16[8,2,32,128]{3,2,1,0:T(8,128)(2,1)} %copy-done.4) | copy-start | bytes 393220

commit v2 on v1

--- a/solution.py
+++ b/solution.py
@@ -32,31 +32,6 @@
         out_specs=VMEM,
         out_shape=jax.ShapeDtypeStruct((groups, 2, rows, HEAD), keys.dtype),
     )(keys, values)
-
-
-def outgoing_kernel(shifts, position_ref, own_ref, near_ref, far_ref, *out_refs):
-    y = lax.rem(position_ref[0], WIDE)
-    for shift, out in zip(shifts, out_refs):
-        out[0] = near_ref[...]
-        target = lax.rem(y + shift, WIDE)
-
-        @pl.when(y < target)
-        def _():
-            out[1] = own_ref[...]
-
-        @pl.when(y > target)
-        def _():
-            out[1] = far_ref[...]
-
-
-def outgoing(position, own, near, far, shifts):
-    shape = jax.ShapeDtypeStruct((2, *own.shape), own.dtype)
-    return pl.pallas_call(
-        functools.partial(outgoing_kernel, shifts),
-        in_specs=[SMEM, VMEM, VMEM, VMEM],
-        out_specs=[VMEM] * len(shifts),
-        out_shape=[shape] * len(shifts),
-    )(position, own, near, far)
 
 
 def attend_kernel(plan, per_item, own, has_state, final, *refs):
@@ -242,24 +217,24 @@
             block, "ctx", [(i, i - i % WIDE + (i + shift) % WIDE) for i in range(blocks)]
         )
 
+    y = lax.rem(position[0], WIDE)
     near = back(own, WIDE)
-    far = back(own, 2 * WIDE)
     state = attend(position, queries, segments, [own], [(0, None, own_block)], 1, own=True)
     shifts = (1, 3, 2)
-    arrived = [
-        around(block, shift)
-        for block, shift in zip(outgoing(position, own, near, far, shifts), shifts)
+    near_arrived = [around(near, shift) for shift in shifts]
+    far = back(near, WIDE)
+    edge_arrived = [
+        around(jnp.where(y < lax.rem(y + shift, WIDE), own, far), shift) for shift in shifts
     ]
     plan = [
         (0, None, functools.partial(back_block, WIDE)),
         (1, None, functools.partial(back_block, 2 * WIDE)),
     ]
     state = attend(position, queries, segments, [near, far], plan, 2, state=state)
-    plan = []
-    for i, shift in enumerate(shifts):
-        plan.append((i, 0, functools.partial(near_row, shift)))
-        plan.append((i, 1, functools.partial(edge_row, shift)))
-    return attend(position, queries, segments, arrived, plan, 3, state=state, final=True)
+    plan = [(i, None, functools.partial(near_row, shift)) for i, shift in enumerate(shifts)]
+    state = attend(position, queries, segments, near_arrived, plan, 3, state=state)
+    plan = [(i, None, functools.partial(edge_row, shift)) for i, shift in enumerate(shifts)]
+    return attend(position, queries, segments, edge_arrived, plan, 3, state=state, final=True)
 
 
 def solution(mesh):

time: 50.2 us -> 43.1 us (0.86)
  the two profiles are of different devices: /device:TPU:8 before, /device:TPU:96 now
where the time goes in v2:
time: 43.1 us; the launch traced here: 42.9 us
  starting transfers between devices  17.6 us (41%)
  Pallas kernels  12 us (28%)
  blocking collectives  10.6 us (25%)
  waiting for transfers between devices  2.58 us (6%)
    ppermute x6, starting transfers between devices, around(): lax.ppermute(block, 'ctx', [(i, i - i % WIDE + (i + shift) % WIDE) for i...  10.8 us
    all_to_all x1, blocking collectives, on_device(): lax.all_to_all(pack(keys, values), 'kvg', split_axis=0, concat_axis=0, ti...  10.6 us
    pallas_call x4, Pallas kernels, attend(): pl.pallas_call(functools.partial(attend_kernel, plan, per_item, own, bool...  10.4 us
    ppermute x2, starting transfers between devices, back(): lax.ppermute(block, 'ctx', [(i, (i + distance) % blocks) for i in range(b...  6.82 us
    ppermute x2, waiting for transfers between devices, back(): lax.ppermute(block, 'ctx', [(i, (i + distance) % blocks) for i in range(b...  2.57 us
    pallas_call x1, Pallas kernels, pack(): pl.pallas_call(functools.partial(pack_kernel, groups), in_specs=[VMEM, VM...  1.56 us
  transfers between devices with their start and end apart: 8, of which 1 were waited for; matrix products, arithmetic and copies ran while one was open for 0% of the time, Pallas kernels for 16%

profile of v2, /device:TPU:96, one launch (start us, length us, event | category | flops | bytes accessed | tf_op | source)
XLA Modules:
  0.0 42.9 jit_solution(5174663968149346637)
XLA Ops:
  0.0 0.0 copy-start.1
  0.0 1.6 %shard_map.46 = bf16[8,2,32,128]{3,2,1,0:T(8,128)(2,1)} custom-call(bf16[32,1024]{1,0:T(8,128)(2,1)} %k_ref.1, bf16[32,1024]{1,0:T(8,128)(2,1)} %v_ref.1), custom_call_target="tpu_custom_call" | custom-call | tf_op jit(solution)/shard_map/pallas_call | solution.py:29
  1.6 0.0 copy-start
  1.6 10.6 %all_to_all.5.refs_3_ = bf16[8,2,32,128]{3,2,1,0:T(8,128)(2,1)S(1)} all-to-all(bf16[8,2,32,128]{3,2,1,0:T(8,128)(2,1)} %shard_map.46), channel_id=1, replica_groups=mesh['ctx'=32,'kvg'=8] {'kvg'}, dimensions={0} | all-to-all | bytes 262144 | tf_op jit(solution)/shard_map/all_to_all | solution.py:210
  12.1 3.1 %collective-permute-start = (bf16[8,2,32,128]{3,2,1,0:T(8,128)(2,1)S(1)}, bf16[8,2,32,128]{3,2,1,0:T(8,128)(2,1)S(1)}, u32[]{:S(2)}, u32[]{:S(2)}) collective-permute-start(bf16[8,2,32,128]{3,2,1,0:T(8,128)(2,1)S(1)} %all_to_all.5.refs_3_), channel_id=1, source_target_pairs={{0,32},{8,40},{16,48},{24,56},{32,64},{40,72},{48,80},{56,88},{64,... | collective-permute-start | bytes 393224 | tf_op jit(solution)/shard_map/ppermute | solution.py:213
  15.3 2.6 %collective-permute-done.refs_3_ = bf16[8,2,32,128]{3,2,1,0:T(8,128)(2,1)S(1)} collective-permute-done((bf16[8,2,32,128]{3,2,1,0:T(8,128)(2,1)S(1)}, bf16[8,2,32,128]{3,2,1,0:T(8,128)(2,1)S(1)}, u32[]{:S(2)}, u32[]{:S(2)}) %collective-permute-start) | collective-permute-done | bytes 131104 | tf_op jit(solution)/shard_map/ppermute | solution.py:213
  17.8 3.7 %collective-permute-start.1 = (bf16[8,2,32,128]{3,2,1,0:T(8,128)(2,1)S(1)}, bf16[8,2,32,128]{3,2,1,0:T(8,128)(2,1)S(1)}, u32[]{:S(2)}, u32[]{:S(2)}) collective-permute-start(bf16[8,2,32,128]{3,2,1,0:T(8,128)(2,1)S(1)} %collective-permute-done.refs_3_), channel_id=1, source_target_pairs={{0,32},{8,40},{16,48},{24,56},{32,64},{40,72},{48,80},{56,88},{64,... | collective-permute-start | bytes 393224 | tf_op jit(solution)/shard_map/ppermute | solution.py:213
  21.5 0.0 copy-done.1
  21.6 1.7 %collective-permute-start.5 = (bf16[8,2,32,128]{3,2,1,0:T(8,128)(2,1)S(1)}, bf16[8,2,32,128]{3,2,1,0:T(8,128)(2,1)S(1)}, u32[]{:S(2)}, u32[]{:S(2)}) collective-permute-start(bf16[8,2,32,128]{3,2,1,0:T(8,128)(2,1)S(1)} %collective-permute-done.refs_3_), channel_id=1, source_target_pairs={{0,8},{8,16},{16,24},{24,0},{32,40},{40,48},{48,56},{56,32},{64,72... | collective-permute-start | bytes 393224 | tf_op jit(solution)/shard_map/ppermute | solution.py:216
  23.2 1.7 %collective-permute-start.6 = (bf16[8,2,32,128]{3,2,1,0:T(8,128)(2,1)S(1)}, bf16[8,2,32,128]{3,2,1,0:T(8,128)(2,1)S(1)}, u32[]{:S(2)}, u32[]{:S(2)}) collective-permute-start(bf16[8,2,32,128]{3,2,1,0:T(8,128)(2,1)S(1)} %collective-permute-done.refs_3_), channel_id=1, source_target_pairs={{0,24},{8,0},{16,8},{24,16},{32,56},{40,32},{48,40},{56,48},{64,88... | collective-permute-start | bytes 393224 | tf_op jit(solution)/shard_map/ppermute | solution.py:216
  24.9 2.0 %collective-permute-start.7 = (bf16[8,2,32,128]{3,2,1,0:T(8,128)(2,1)S(1)}, bf16[8,2,32,128]{3,2,1,0:T(8,128)(2,1)S(1)}, u32[]{:S(2)}, u32[]{:S(2)}) collective-permute-start(bf16[8,2,32,128]{3,2,1,0:T(8,128)(2,1)S(1)} %collective-permute-done.refs_3_), channel_id=1, source_target_pairs={{0,16},{8,24},{16,0},{24,8},{32,48},{40,56},{48,32},{56,40},{64,80... | collective-permute-start | bytes 393224 | tf_op jit(solution)/shard_map/ppermute | solution.py:216
  26.9 0.0 collective-permute-done.1.refs_4_
  26.9 0.8 %collective-permute-start.2 = (bf16[8,2,32,128]{3,2,1,0:T(8,128)(2,1)S(1)}, bf16[8,2,32,128]{3,2,1,0:T(8,128)(2,1)S(1)}, u32[]{:S(2)}, u32[]{:S(2)}) collective-permute-start(bf16[8,2,32,128]{3,2,1,0:T(8,128)(2,1)S(1)} %get-tuple-element.19), channel_id=1, source_target_pairs={{0,8},{8,16},{16,24},{24,0},{32,40},{40,48},{48,56},{56,32},{64,72... | collective-permute-start | bytes 393224 | tf_op jit(solution)/shard_map/ppermute | solution.py:216
  27.6 2.6 %collective-permute-start.3 = (bf16[8,2,32,128]{3,2,1,0:T(8,128)(2,1)S(1)}, bf16[8,2,32,128]{3,2,1,0:T(8,128)(2,1)S(1)}, u32[]{:S(2)}, u32[]{:S(2)}) collective-permute-start(bf16[8,2,32,128]{3,2,1,0:T(8,128)(2,1)S(1)} %get-tuple-element.18), channel_id=1, source_target_pairs={{0,24},{8,0},{16,8},{24,16},{32,56},{40,32},{48,40},{56,48},{64,88... | collective-permute-start | bytes 393224 | tf_op jit(solution)/shard_map/ppermute | solution.py:216
  30.2 0.0 collective-permute-done.5.refs_3_
  30.2 2.2 %collective-permute-start.4 = (bf16[8,2,32,128]{3,2,1,0:T(8,128)(2,1)S(1)}, bf16[8,2,32,128]{3,2,1,0:T(8,128)(2,1)S(1)}, u32[]{:S(2)}, u32[]{:S(2)}) collective-permute-start(bf16[8,2,32,128]{3,2,1,0:T(8,128)(2,1)S(1)} %get-tuple-element.17), channel_id=1, source_target_pairs={{0,16},{8,24},{16,0},{24,8},{32,48},{40,56},{48,32},{56,40},{64,80... | collective-permute-start | bytes 393224 | tf_op jit(solution)/shard_map/ppermute | solution.py:216
  32.4 0.0 copy-done
  32.4 1.5 %shard_map.47 = (f32[8,128,256]{2,1,0:T(8,128)S(1)}, f32[8,8,256]{2,1,0:T(8,128)S(1)}) custom-call(s32[1]{0:T(128)} %bitcast.refs_0_, bf16[256,1024]{1,0:T(8,128)(2,1)S(1)} %copy-done, s32[32,256]{1,0:T(8,128)S(1)} %reshape.7.refs_2_, bf16[8,2,32,128]{3,2,1,0:T(8,128)(2,1)S(1)} %all_to_all.5.refs_3_), custom_call_target="tpu_custom_call" | custom-call | flops 268435456 | bytes 1048576 | tf_op jit(solution)/shard_map/pallas_call | solution.py:162
  33.9 2.3 %shard_map.48 = (f32[8,128,256]{2,1,0:T(8,128)S(1)}, f32[8,8,256]{2,1,0:T(8,128)S(1)}) custom-call(s32[1]{0:T(128)} %bitcast.refs_0_, bf16[256,1024]{1,0:T(8,128)(2,1)S(1)} %copy-done, s32[32,256]{1,0:T(8,128)S(1)} %reshape.7.refs_2_, bf16[8,2,32,128]{3,2,1,0:T(8,128)(2,1)S(1)} %collective-permute-done.refs_3_, ...), custom_call_target="tpu_custom_call" | custom-call | flops 536870912 | bytes 1048576 | tf_op jit(solution)/shard_map/pallas_call | solution.py:162
  36.2 0.0 collective-permute-done.6.refs_4_
  36.2 0.0 collective-permute-done.7.refs_5_
  36.2 2.9 %shard_map.49 = (f32[8,128,256]{2,1,0:T(8,128)S(1)}, f32[8,8,256]{2,1,0:T(8,128)S(1)}) custom-call(s32[1]{0:T(128)} %bitcast.refs_0_, bf16[256,1024]{1,0:T(8,128)(2,1)S(1)} %copy-done, s32[32,256]{1,0:T(8,128)S(1)} %reshape.7.refs_2_, bf16[8,2,32,128]{3,2,1,0:T(8,128)(2,1)S(1)} %collective-permute-done.5.refs_3_, ...), custom_call_target="tpu_custom_call" | custom-call | flops 805306368 | bytes 1048576 | tf_op jit(solution)/shard_map/pallas_call | solution.py:162
  39.2 0.0 collective-permute-done.2.refs_3_
  39.2 0.0 collective-permute-done.3.refs_4_
  39.2 0.0 collective-permute-done.4.refs_5_
  39.2 3.7 %shard_map.50 = bf16[256,1024]{1,0:T(8,128)(2,1)} custom-call(s32[1]{0:T(128)} %bitcast.refs_0_, bf16[256,1024]{1,0:T(8,128)(2,1)S(1)} %copy-done, s32[32,256]{1,0:T(8,128)S(1)} %reshape.7.refs_2_, bf16[8,2,32,128]{3,2,1,0:T(8,128)(2,1)S(1)} %collective-permute-done.2.refs_3_, bf16[8,2,32,128]{3,2,1,0:T(8,128)(2,1)S(1)} %collective-permute-done.3.refs_4_, ...), custom_call_target="tpu_custom_call" | custom-call | flops 805306368 | bytes 1048576 | tf_op jit(solution)/shard_map/pallas_call | solution.py:162
  (2 shorter events, 0.0 us)
Async XLA Ops:
  0.0 21.5 %copy-start.1 = (s32[8192]{0:T(1024)S(1)}, s32[8192]{0:T(1024)}, u32[]{:S(2)}) copy-start(s32[8192]{0:T(1024)} %param.7) | copy-start | bytes 98308
  1.6 30.8 %copy-start = (bf16[256,1024]{1,0:T(8,128)(2,1)S(1)}, bf16[256,1024]{1,0:T(8,128)(2,1)}, u32[]{:S(2)}) copy-start(bf16[256,1024]{1,0:T(8,128)(2,1)} %refs_1_.7) | copy-start | bytes 1572868
  12.1 5.7 %collective-permute-start = (bf16[8,2,32,128]{3,2,1,0:T(8,128)(2,1)S(1)}, bf16[8,2,32,128]{3,2,1,0:T(8,128)(2,1)S(1)}, u32[]{:S(2)}, u32[]{:S(2)}) collective-permute-start(bf16[8,2,32,128]{3,2,1,0:T(8,128)(2,1)S(1)} %all_to_all.5.refs_3_), channel_id=1, source_target_pairs={{0,32},{8,40},{16,48},{24,56},{32,64},{40,72},{48,80},{56,88},{64,... | collective-permute-start | bytes 393224 | tf_op jit(solution)/shard_map/ppermute | solution.py:213
  17.8 9.0 %collective-permute-start.1 = (bf16[8,2,32,128]{3,2,1,0:T(8,128)(2,1)S(1)}, bf16[8,2,32,128]{3,2,1,0:T(8,128)(2,1)S(1)}, u32[]{:S(2)}, u32[]{:S(2)}) collective-permute-start(bf16[8,2,32,128]{3,2,1,0:T(8,128)(2,1)S(1)} %collective-permute-done.refs_3_), channel_id=1, source_target_pairs={{0,32},{8,40},{16,48},{24,56},{32,64},{40,72},{48,80},{56,88},{64,... | collective-permute-start | bytes 393224 | tf_op jit(solution)/shard_map/ppermute | solution.py:213
  21.6 8.7 %collective-permute-start.5 = (bf16[8,2,32,128]{3,2,1,0:T(8,128)(2,1)S(1)}, bf16[8,2,32,128]{3,2,1,0:T(8,128)(2,1)S(1)}, u32[]{:S(2)}, u32[]{:S(2)}) collective-permute-start(bf16[8,2,32,128]{3,2,1,0:T(8,128)(2,1)S(1)} %collective-permute-done.refs_3_), channel_id=1, source_target_pairs={{0,8},{8,16},{16,24},{24,0},{32,40},{40,48},{48,56},{56,32},{64,72... | collective-permute-start | bytes 393224 | tf_op jit(solution)/shard_map/ppermute | solution.py:216
  23.2 13.0 %collective-permute-start.6 = (bf16[8,2,32,128]{3,2,1,0:T(8,128)(2,1)S(1)}, bf16[8,2,32,128]{3,2,1,0:T(8,128)(2,1)S(1)}, u32[]{:S(2)}, u32[]{:S(2)}) collective-permute-start(bf16[8,2,32,128]{3,2,1,0:T(8,128)(2,1)S(1)} %collective-permute-done.refs_3_), channel_id=1, source_target_pairs={{0,24},{8,0},{16,8},{24,16},{32,56},{40,32},{48,40},{56,48},{64,88... | collective-permute-start | bytes 393224 | tf_op jit(solution)/shard_map/ppermute | solution.py:216
  24.9 11.4 %collective-permute-start.7 = (bf16[8,2,32,128]{3,2,1,0:T(8,128)(2,1)S(1)}, bf16[8,2,32,128]{3,2,1,0:T(8,128)(2,1)S(1)}, u32[]{:S(2)}, u32[]{:S(2)}) collective-permute-start(bf16[8,2,32,128]{3,2,1,0:T(8,128)(2,1)S(1)} %collective-permute-done.refs_3_), channel_id=1, source_target_pairs={{0,16},{8,24},{16,0},{24,8},{32,48},{40,56},{48,32},{56,40},{64,80... | collective-permute-start | bytes 393224 | tf_op jit(solution)/shard_map/ppermute | solution.py:216
  26.9 12.3 %collective-permute-start.2 = (bf16[8,2,32,128]{3,2,1,0:T(8,128)(2,1)S(1)}, bf16[8,2,32,128]{3,2,1,0:T(8,128)(2,1)S(1)}, u32[]{:S(2)}, u32[]{:S(2)}) collective-permute-start(bf16[8,2,32,128]{3,2,1,0:T(8,128)(2,1)S(1)} %get-tuple-element.19), channel_id=1, source_target_pairs={{0,8},{8,16},{16,24},{24,0},{32,40},{40,48},{48,56},{56,32},{64,72... | collective-permute-start | bytes 393224 | tf_op jit(solution)/shard_map/ppermute | solution.py:216
  27.6 11.5 %collective-permute-start.3 = (bf16[8,2,32,128]{3,2,1,0:T(8,128)(2,1)S(1)}, bf16[8,2,32,128]{3,2,1,0:T(8,128)(2,1)S(1)}, u32[]{:S(2)}, u32[]{:S(2)}) collective-permute-start(bf16[8,2,32,128]{3,2,1,0:T(8,128)(2,1)S(1)} %get-tuple-element.18), channel_id=1, source_target_pairs={{0,24},{8,0},{16,8},{24,16},{32,56},{40,32},{48,40},{56,48},{64,88... | collective-permute-start | bytes 393224 | tf_op jit(solution)/shard_map/ppermute | solution.py:216
  30.2 9.0 %collective-permute-start.4 = (bf16[8,2,32,128]{3,2,1,0:T(8,128)(2,1)S(1)}, bf16[8,2,32,128]{3,2,1,0:T(8,128)(2,1)S(1)}, u32[]{:S(2)}, u32[]{:S(2)}) collective-permute-start(bf16[8,2,32,128]{3,2,1,0:T(8,128)(2,1)S(1)} %get-tuple-element.17), channel_id=1, source_target_pairs={{0,16},{8,24},{16,0},{24,8},{32,48},{40,56},{48,32},{56,40},{64,80... | collective-permute-start | bytes 393224 | tf_op jit(solution)/shard_map/ppermute | solution.py:216

commit v3 on v2

--- a/solution.py
+++ b/solution.py
@@ -49,19 +49,20 @@
     else:
         acc_out, stat_out = refs[:2]
         refs = refs[2:]
-    k_s, vt_s, bias_s, s_s, p_s, t_s, acc_s = refs
+    k_s, vt_s, bias_s, one_s, s_s, p_s, t_s, acc_s, *rest = refs
 
     rows = q_ref.shape[0]
     heads = q_ref.shape[1] // HEAD
     count = len(plan)
     c = position_ref[0]
-    q_seg = seg_ref[pl.ds(c, 1), :]
+    parts = rows // HEAD
+    q_seg = jnp.concatenate([seg_ref[pl.ds(parts * c + i, 1), :] for i in range(parts)], 1)
     first_seg = jnp.min(q_seg)
     start = jnp.sum((seg_ref[...] < first_seg).astype(jnp.int32))
     query_bias = jnp.where(q_seg == first_seg, 0.0, MASKED).astype(jnp.float32)
     for i, (b, slot, block_of) in enumerate(plan):
         src = kv_refs[b] if slot is None else kv_refs[b].at[slot]
-        k_s[i * rows : (i + 1) * rows] = src[:, 0].reshape(rows, HEAD)
+        k_s[i * rows : (i + 1) * rows, :HEAD] = src[:, 0].reshape(rows, HEAD)
         vt_s[:, i * rows : (i + 1) * rows] = src[:, 1].reshape(rows, HEAD).T
         if own:
             key_seg = jnp.broadcast_to(q_seg.astype(jnp.float32), (rows, rows)).T
@@ -70,19 +71,25 @@
             allowed = (key_seg == q_seg.astype(jnp.float32)) & (k_pos <= q_pos)
             bias_s[...] = jnp.where(allowed, 0.0, MASKED).astype(jnp.float32)
         else:
+            lane = lax.broadcasted_iota(jnp.int32, (rows, HEAD), 1)
             k_pos = block_of(c) * rows + lax.broadcasted_iota(jnp.int32, (rows, HEAD), 0)
-            bias_s[i * rows : (i + 1) * rows] = jnp.where(k_pos >= start, 0.0, MASKED).astype(
-                jnp.float32
+            masked = (k_pos < start) & (lane == 0)
+            k_s[i * rows : (i + 1) * rows, HEAD:] = jnp.where(masked, MASKED, 0.0).astype(
+                jnp.bfloat16
             )
+            one_s[...] = jnp.where(lane == 0, 1.0, 0.0).astype(jnp.bfloat16)
 
     splits = count // per_item
     items = [(h, g) for h in range(heads) for g in range(splits)]
 
     def score(t):
         h, g = items[t]
+        q = q_ref[:, h * HEAD : (h + 1) * HEAD]
+        if not own:
+            q = jnp.concatenate([q, one_s[...]], 1)
         s_s[t % 2] = lax.dot_general(
             k_s[g * per_item * rows : (g + 1) * per_item * rows],
-            q_ref[:, h * HEAD : (h + 1) * HEAD],
+            q,
             NT,
             preferred_element_type=jnp.float32,
         )
@@ -91,9 +98,8 @@
         _, g = items[t]
         for i in range(per_item):
             x = s_s[t % 2, i * rows : (i + 1) * rows]
-            at = (g * per_item + i) * rows
-            bias = bias_s[at : at + rows]
-            x = x + (bias if own else jnp.concatenate([bias] * (rows // HEAD), 1))
+            if own:
+                x = x + bias_s[...]
             top = jnp.max(x, 0, keepdims=True)
             expo = jnp.exp2((x - top) * EXP2_SCALE)
             t_s[t % 2, i : i + 1] = top if own else top + query_bias
@@ -131,19 +137,29 @@
             t_s[2 + h % 2, 0:1] = best
             t_s[2 + h % 2, 8:9] = total
         elif final:
-            out_ref[:, h * HEAD : (h + 1) * HEAD] = (acc / total).T.astype(jnp.bfloat16)
+            out_s, sems = rest
+            out_s[h] = (acc / total).astype(jnp.bfloat16).T
+            copies.append(
+                pltpu.make_async_copy(
+                    out_s.at[h], out_ref.at[:, h * HEAD : (h + 1) * HEAD], sems.at[h]
+                )
+            )
+            copies[-1].start()
         else:
             acc_out[h] = acc
             stat_out[h, 0:1] = best
             stat_out[h, 1:2] = total
 
+    copies = []
     for t in range(len(items) + 2):
+        if t < len(items):
+            score(t)
+        if 1 <= t <= len(items):
+            soften(t - 1)
         if t >= 2:
             mix(t - 2)
-        if 1 <= t <= len(items):
-            soften(t - 1)
-        if t < len(items):
-            score(t)
+    for copy in copies:
+        copy.wait()
 
 
 def attend(position, queries, segments, buffers, plan, per_item, own=False, state=(), final=False):
@@ -152,7 +168,7 @@
     count = len(plan)
     if final:
         out_shape = jax.ShapeDtypeStruct(queries.shape, queries.dtype)
-        out_specs = VMEM
+        out_specs = pl.BlockSpec(memory_space=pl.ANY)
     else:
         out_shape = [
             jax.ShapeDtypeStruct((heads, HEAD, rows), jnp.float32),
@@ -165,14 +181,20 @@
         out_specs=out_specs,
         out_shape=out_shape,
         scratch_shapes=[
-            pltpu.VMEM((count * rows, HEAD), jnp.bfloat16),
+            pltpu.VMEM((count * rows, HEAD if own else 2 * HEAD), jnp.bfloat16),
             pltpu.VMEM((HEAD, count * rows), jnp.bfloat16),
-            pltpu.VMEM((count * rows, rows if own else HEAD), jnp.float32),
+            pltpu.VMEM((rows, rows if own else HEAD), jnp.float32),
+            pltpu.VMEM((rows, HEAD), jnp.bfloat16),
             pltpu.VMEM((2, per_item * rows, rows), jnp.float32),
             pltpu.VMEM((2, per_item * rows, rows), jnp.bfloat16),
             pltpu.VMEM((4, 16, rows), jnp.float32),
             pltpu.VMEM((2, HEAD, rows), jnp.float32),
-        ],
+        ]
+        + (
+            [pltpu.VMEM((heads, rows, HEAD), queries.dtype), pltpu.SemaphoreType.DMA((heads,))]
+            if final
+            else []
+        ),
         compiler_params=pltpu.CompilerParams(vmem_limit_bytes=24 << 20),
         cost_estimate=pl.CostEstimate(
             flops=4 * heads * rows * rows * HEAD * count,
@@ -206,7 +228,7 @@
     rows = queries.shape[0]
     blocks = lax.axis_size("ctx")
     position = lax.axis_index("ctx").astype(jnp.int32).reshape(1)
-    segments = segment_ids.reshape(blocks, rows)
+    segments = segment_ids.reshape(-1, HEAD)
     own = lax.all_to_all(pack(keys, values), "kvg", split_axis=0, concat_axis=0, tiled=True)
 
     def back(block, distance):
@@ -220,6 +242,7 @@
     y = lax.rem(position[0], WIDE)
     near = back(own, WIDE)
     state = attend(position, queries, segments, [own], [(0, None, own_block)], 1, own=True)
+    near, state = lax.optimization_barrier((near, state))
     shifts = (1, 3, 2)
     near_arrived = [around(near, shift) for shift in shifts]
     far = back(near, WIDE)
@@ -230,9 +253,8 @@
         (0, None, functools.partial(back_block, WIDE)),
         (1, None, functools.partial(back_block, 2 * WIDE)),
     ]
-    state = attend(position, queries, segments, [near, far], plan, 2, state=state)
-    plan = [(i, None, functools.partial(near_row, shift)) for i, shift in enumerate(shifts)]
-    state = attend(position, queries, segments, near_arrived, plan, 3, state=state)
+    plan += [(2 + i, None, functools.partial(near_row, shift)) for i, shift in enumerate(shifts)]
+    state = attend(position, queries, segments, [near, far, *near_arrived], plan, 5, state=state)
     plan = [(i, None, functools.partial(edge_row, shift)) for i, shift in enumerate(shifts)]
     return attend(position, queries, segments, edge_arrived, plan, 3, state=state, final=True)
 

time: 43.1 us -> 40.9 us (0.949)
  Pallas kernels: 12 us -> 10.2 us
  waiting for transfers between devices: 2.58 us -> 1.26 us
  local copies, waits for them, and re-layouts: 0.02 us -> 0.77 us
    ppermute x2, waiting for transfers between devices: 2.57 us -> 0.51 us  [back(): lax.ppermute(block, 'ctx', [(i, (i + distance) % blocks) for i in range(b...]
    pallas_call x4 -> x3, Pallas kernels: 10.4 us -> 8.58 us  [attend(): pl.pallas_call(functools.partial(attend_kernel, plan, per_item, own, bool...]
    unnamed x4 -> x6, local copies, waits for them, and re-layouts: 0.01 us -> 0.77 us
    ppermute x6, waiting for transfers between devices: 0.02 us -> 0.75 us  [around(): lax.ppermute(block, 'ctx', [(i, i - i % WIDE + (i + shift) % WIDE) for i...]
  transfers between devices with their start and end apart: 8 -> 8, of which waited for: 1 -> 2; matrix products, arithmetic and copies ran while one was open for 0% -> 0% of each run, Pallas kernels for 16% -> 13%
where the time goes in v3:
time: 40.9 us; the launch traced here: 40.6 us
  starting transfers between devices  17.7 us (43%)
  blocking collectives  10.4 us (25%)
  Pallas kernels  10.2 us (25%)
  waiting for transfers between devices  1.26 us (3%)
  local copies, waits for them, and re-layouts  0.77 us (2%)
    ppermute x6, starting transfers between devices, around(): lax.ppermute(block, 'ctx', [(i, i - i % WIDE + (i + shift) % WIDE) for i...  10.9 us
    all_to_all x1, blocking collectives, on_device(): lax.all_to_all(pack(keys, values), 'kvg', split_axis=0, concat_axis=0, ti...  10.4 us
    pallas_call x3, Pallas kernels, attend(): pl.pallas_call(functools.partial(attend_kernel, plan, per_item, own, bool...  8.58 us
    ppermute x2, starting transfers between devices, back(): lax.ppermute(block, 'ctx', [(i, (i + distance) % blocks) for i in range(b...  6.82 us
    pallas_call x1, Pallas kernels, pack(): pl.pallas_call(functools.partial(pack_kernel, groups), in_specs=[VMEM, VM...  1.61 us
  transfers between devices with their start and end apart: 8, of which 2 were waited for; matrix products, arithmetic and copies ran while one was open for 0% of the time, Pallas kernels for 13%

profile of v3, /device:TPU:96, one launch (start us, length us, event | category | flops | bytes accessed | tf_op | source)
XLA Modules:
  0.0 40.6 jit_solution(5795050115028668248)
XLA Ops:
  0.0 0.0 copy-start
  0.0 1.6 %shard_map.46 = bf16[8,2,32,128]{3,2,1,0:T(8,128)(2,1)} custom-call(bf16[32,1024]{1,0:T(8,128)(2,1)} %k_ref.1, bf16[32,1024]{1,0:T(8,128)(2,1)} %v_ref.1), custom_call_target="tpu_custom_call" | custom-call | tf_op jit(solution)/shard_map/pallas_call | solution.py:29
  1.6 10.4 %all_to_all.5.refs_3_ = bf16[8,2,32,128]{3,2,1,0:T(8,128)(2,1)S(1)} all-to-all(bf16[8,2,32,128]{3,2,1,0:T(8,128)(2,1)} %shard_map.46), channel_id=1, replica_groups=mesh['ctx'=32,'kvg'=8] {'kvg'}, dimensions={0} | all-to-all | bytes 262144 | tf_op jit(solution)/shard_map/all_to_all | solution.py:232
  12.0 3.1 %collective-permute-start = (bf16[8,2,32,128]{3,2,1,0:T(8,128)(2,1)S(1)}, bf16[8,2,32,128]{3,2,1,0:T(8,128)(2,1)S(1)}, u32[]{:S(2)}, u32[]{:S(2)}) collective-permute-start(bf16[8,2,32,128]{3,2,1,0:T(8,128)(2,1)S(1)} %all_to_all.5.refs_3_), channel_id=1, source_target_pairs={{0,32},{8,40},{16,48},{24,56},{32,64},{40,72},{48,80},{56,88},{64,... | collective-permute-start | bytes 393224 | tf_op jit(solution)/shard_map/ppermute | solution.py:235
  15.2 0.0 copy-done
  15.2 0.0 copy-start.1
  15.2 0.8 %copy-done.1 = s32[8192]{0:T(1024)S(1)} copy-done((s32[8192]{0:T(1024)S(1)}, s32[8192]{0:T(1024)}, u32[]{:S(2)}) %copy-start.1) | copy-done | bytes 32792
  15.9 1.3 %shard_map.47 = (f32[8,128,256]{2,1,0:T(8,128)S(1)}, f32[8,8,256]{2,1,0:T(8,128)S(1)}) custom-call(s32[1]{0:T(128)} %bitcast.refs_0_, bf16[256,1024]{1,0:T(8,128)(2,1)S(1)} %copy-done, s32[64,128]{1,0:T(8,128)S(1)} %bitcast.2, bf16[8,2,32,128]{3,2,1,0:T(8,128)(2,1)S(1)} %all_to_all.5.refs_3_), custom_call_target="tpu_custom_call" | custom-call | flops 268435456 | bytes 1048576 | tf_op jit(solution)/shard_map/pallas_call | solution.py:178
  17.2 0.5 %collective-permute-done.refs_3_ = bf16[8,2,32,128]{3,2,1,0:T(8,128)(2,1)S(1)} collective-permute-done((bf16[8,2,32,128]{3,2,1,0:T(8,128)(2,1)S(1)}, bf16[8,2,32,128]{3,2,1,0:T(8,128)(2,1)S(1)}, u32[]{:S(2)}, u32[]{:S(2)}) %collective-permute-start) | collective-permute-done | bytes 131104 | tf_op jit(solution)/shard_map/ppermute | solution.py:235
  17.7 3.7 %collective-permute-start.1 = (bf16[8,2,32,128]{3,2,1,0:T(8,128)(2,1)S(1)}, bf16[8,2,32,128]{3,2,1,0:T(8,128)(2,1)S(1)}, u32[]{:S(2)}, u32[]{:S(2)}) collective-permute-start(bf16[8,2,32,128]{3,2,1,0:T(8,128)(2,1)S(1)} %collective-permute-done.refs_3_), channel_id=1, source_target_pairs={{0,32},{8,40},{16,48},{24,56},{32,64},{40,72},{48,80},{56,88},{64,... | collective-permute-start | bytes 393224 | tf_op jit(solution)/shard_map/ppermute | solution.py:235
  21.4 0.0 copy-start.2
  21.4 1.6 %collective-permute-start.5 = (bf16[8,2,32,128]{3,2,1,0:T(8,128)(2,1)S(1)}, bf16[8,2,32,128]{3,2,1,0:T(8,128)(2,1)S(1)}, u32[]{:S(2)}, u32[]{:S(2)}) collective-permute-start(bf16[8,2,32,128]{3,2,1,0:T(8,128)(2,1)S(1)} %collective-permute-done.refs_3_), channel_id=1, source_target_pairs={{0,8},{8,16},{16,24},{24,0},{32,40},{40,48},{48,56},{56,32},{64,72... | collective-permute-start | bytes 393224 | tf_op jit(solution)/shard_map/ppermute | solution.py:238
  23.0 1.7 %collective-permute-start.6 = (bf16[8,2,32,128]{3,2,1,0:T(8,128)(2,1)S(1)}, bf16[8,2,32,128]{3,2,1,0:T(8,128)(2,1)S(1)}, u32[]{:S(2)}, u32[]{:S(2)}) collective-permute-start(bf16[8,2,32,128]{3,2,1,0:T(8,128)(2,1)S(1)} %collective-permute-done.refs_3_), channel_id=1, source_target_pairs={{0,24},{8,0},{16,8},{24,16},{32,56},{40,32},{48,40},{56,48},{64,88... | collective-permute-start | bytes 393224 | tf_op jit(solution)/shard_map/ppermute | solution.py:238
  24.7 2.0 %collective-permute-start.7 = (bf16[8,2,32,128]{3,2,1,0:T(8,128)(2,1)S(1)}, bf16[8,2,32,128]{3,2,1,0:T(8,128)(2,1)S(1)}, u32[]{:S(2)}, u32[]{:S(2)}) collective-permute-start(bf16[8,2,32,128]{3,2,1,0:T(8,128)(2,1)S(1)} %collective-permute-done.refs_3_), channel_id=1, source_target_pairs={{0,16},{8,24},{16,0},{24,8},{32,48},{40,56},{48,32},{56,40},{64,80... | collective-permute-start | bytes 393224 | tf_op jit(solution)/shard_map/ppermute | solution.py:238
  26.7 0.0 collective-permute-done.1.refs_4_
  26.7 0.8 %collective-permute-start.2 = (bf16[8,2,32,128]{3,2,1,0:T(8,128)(2,1)S(1)}, bf16[8,2,32,128]{3,2,1,0:T(8,128)(2,1)S(1)}, u32[]{:S(2)}, u32[]{:S(2)}) collective-permute-start(bf16[8,2,32,128]{3,2,1,0:T(8,128)(2,1)S(1)} %get-tuple-element.21), channel_id=1, source_target_pairs={{0,8},{8,16},{16,24},{24,0},{32,40},{40,48},{48,56},{56,32},{64,72... | collective-permute-start | bytes 393224 | tf_op jit(solution)/shard_map/ppermute | solution.py:238
  27.4 2.6 %collective-permute-start.3 = (bf16[8,2,32,128]{3,2,1,0:T(8,128)(2,1)S(1)}, bf16[8,2,32,128]{3,2,1,0:T(8,128)(2,1)S(1)}, u32[]{:S(2)}, u32[]{:S(2)}) collective-permute-start(bf16[8,2,32,128]{3,2,1,0:T(8,128)(2,1)S(1)} %get-tuple-element.20), channel_id=1, source_target_pairs={{0,24},{8,0},{16,8},{24,16},{32,56},{40,32},{48,40},{56,48},{64,88... | collective-permute-start | bytes 393224 | tf_op jit(solution)/shard_map/ppermute | solution.py:238
  30.0 0.0 collective-permute-done.5.refs_5_
  30.0 2.4 %collective-permute-start.4 = (bf16[8,2,32,128]{3,2,1,0:T(8,128)(2,1)S(1)}, bf16[8,2,32,128]{3,2,1,0:T(8,128)(2,1)S(1)}, u32[]{:S(2)}, u32[]{:S(2)}) collective-permute-start(bf16[8,2,32,128]{3,2,1,0:T(8,128)(2,1)S(1)} %get-tuple-element.19), channel_id=1, source_target_pairs={{0,16},{8,24},{16,0},{24,8},{32,48},{40,56},{48,32},{56,40},{64,80... | collective-permute-start | bytes 393224 | tf_op jit(solution)/shard_map/ppermute | solution.py:238
  32.4 0.0 collective-permute-done.6.refs_6_
  32.4 0.7 %collective-permute-done.7.refs_7_ = bf16[8,2,32,128]{3,2,1,0:T(8,128)(2,1)S(1)} collective-permute-done((bf16[8,2,32,128]{3,2,1,0:T(8,128)(2,1)S(1)}, bf16[8,2,32,128]{3,2,1,0:T(8,128)(2,1)S(1)}, u32[]{:S(2)}, u32[]{:S(2)}) %collective-permute-start.7) | collective-permute-done | bytes 131104 | tf_op jit(solution)/shard_map/ppermute | solution.py:238
  33.1 0.0 copy-done.2
  33.1 3.8 %shard_map.48 = (f32[8,128,256]{2,1,0:T(8,128)S(1)}, f32[8,8,256]{2,1,0:T(8,128)S(1)}) custom-call(s32[1]{0:T(128)} %bitcast.refs_0_, bf16[256,1024]{1,0:T(8,128)(2,1)S(1)} %copy-done, s32[64,128]{1,0:T(8,128)S(1)} %bitcast.3, bf16[8,2,32,128]{3,2,1,0:T(8,128)(2,1)S(1)} %collective-permute-done.refs_3_, ...), custom_call_target="tpu_custom_call" | custom-call | flops 1342177280 | bytes 1048576 | tf_op jit(solution)/shard_map/pallas_call | solution.py:178
  37.0 0.0 collective-permute-done.2.refs_3_
  37.0 0.0 collective-permute-done.3.refs_4_
  37.0 0.0 collective-permute-done.4.refs_5_
  37.0 3.5 %shard_map.49 = bf16[256,1024]{1,0:T(8,128)(2,1)} custom-call(s32[1]{0:T(128)} %bitcast.refs_0_, bf16[256,1024]{1,0:T(8,128)(2,1)S(1)} %copy-done, s32[64,128]{1,0:T(8,128)S(1)} %bitcast.4, bf16[8,2,32,128]{3,2,1,0:T(8,128)(2,1)S(1)} %collective-permute-done.2.refs_3_, bf16[8,2,32,128]{3,2,1,0:T(8,128)(2,1)S(1)} %collective-permute-done.3.refs_4_, ...), custom_call_target="tpu_custom_call" | custom-call | flops 805306368 | bytes 1048576 | tf_op jit(solution)/shard_map/pallas_call | solution.py:178
  (1 shorter events, 0.0 us)
Async XLA Ops:
  0.0 15.2 %copy-start = (bf16[256,1024]{1,0:T(8,128)(2,1)S(1)}, bf16[256,1024]{1,0:T(8,128)(2,1)}, u32[]{:S(2)}) copy-start(bf16[256,1024]{1,0:T(8,128)(2,1)} %refs_1_.5) | copy-start | bytes 1572868
  12.0 5.7 %collective-permute-start = (bf16[8,2,32,128]{3,2,1,0:T(8,128)(2,1)S(1)}, bf16[8,2,32,128]{3,2,1,0:T(8,128)(2,1)S(1)}, u32[]{:S(2)}, u32[]{:S(2)}) collective-permute-start(bf16[8,2,32,128]{3,2,1,0:T(8,128)(2,1)S(1)} %all_to_all.5.refs_3_), channel_id=1, source_target_pairs={{0,32},{8,40},{16,48},{24,56},{32,64},{40,72},{48,80},{56,88},{64,... | collective-permute-start | bytes 393224 | tf_op jit(solution)/shard_map/ppermute | solution.py:235
  15.2 0.8 %copy-start.1 = (s32[8192]{0:T(1024)S(1)}, s32[8192]{0:T(1024)}, u32[]{:S(2)}) copy-start(s32[8192]{0:T(1024)} %param.7) | copy-start | bytes 98308
  17.7 8.9 %collective-permute-start.1 = (bf16[8,2,32,128]{3,2,1,0:T(8,128)(2,1)S(1)}, bf16[8,2,32,128]{3,2,1,0:T(8,128)(2,1)S(1)}, u32[]{:S(2)}, u32[]{:S(2)}) collective-permute-start(bf16[8,2,32,128]{3,2,1,0:T(8,128)(2,1)S(1)} %collective-permute-done.refs_3_), channel_id=1, source_target_pairs={{0,32},{8,40},{16,48},{24,56},{32,64},{40,72},{48,80},{56,88},{64,... | collective-permute-start | bytes 393224 | tf_op jit(solution)/shard_map/ppermute | solution.py:235
  21.4 11.7 %copy-start.2 = (s32[8192]{0:T(1024)S(1)}, s32[8192]{0:T(1024)}, u32[]{:S(2)}) copy-start(s32[8192]{0:T(1024)} %param.7) | copy-start | bytes 98308
  21.4 8.6 %collective-permute-start.5 = (bf16[8,2,32,128]{3,2,1,0:T(8,128)(2,1)S(1)}, bf16[8,2,32,128]{3,2,1,0:T(8,128)(2,1)S(1)}, u32[]{:S(2)}, u32[]{:S(2)}) collective-permute-start(bf16[8,2,32,128]{3,2,1,0:T(8,128)(2,1)S(1)} %collective-permute-done.refs_3_), channel_id=1, source_target_pairs={{0,8},{8,16},{16,24},{24,0},{32,40},{40,48},{48,56},{56,32},{64,72... | collective-permute-start | bytes 393224 | tf_op jit(solution)/shard_map/ppermute | solution.py:238
  23.0 9.4 %collective-permute-start.6 = (bf16[8,2,32,128]{3,2,1,0:T(8,128)(2,1)S(1)}, bf16[8,2,32,128]{3,2,1,0:T(8,128)(2,1)S(1)}, u32[]{:S(2)}, u32[]{:S(2)}) collective-permute-start(bf16[8,2,32,128]{3,2,1,0:T(8,128)(2,1)S(1)} %collective-permute-done.refs_3_), channel_id=1, source_target_pairs={{0,24},{8,0},{16,8},{24,16},{32,56},{40,32},{48,40},{56,48},{64,88... | collective-permute-start | bytes 393224 | tf_op jit(solution)/shard_map/ppermute | solution.py:238
  24.7 8.5 %collective-permute-start.7 = (bf16[8,2,32,128]{3,2,1,0:T(8,128)(2,1)S(1)}, bf16[8,2,32,128]{3,2,1,0:T(8,128)(2,1)S(1)}, u32[]{:S(2)}, u32[]{:S(2)}) collective-permute-start(bf16[8,2,32,128]{3,2,1,0:T(8,128)(2,1)S(1)} %collective-permute-done.refs_3_), channel_id=1, source_target_pairs={{0,16},{8,24},{16,0},{24,8},{32,48},{40,56},{48,32},{56,40},{64,80... | collective-permute-start | bytes 393224 | tf_op jit(solution)/shard_map/ppermute | solution.py:238
  26.7 10.3 %collective-permute-start.2 = (bf16[8,2,32,128]{3,2,1,0:T(8,128)(2,1)S(1)}, bf16[8,2,32,128]{3,2,1,0:T(8,128)(2,1)S(1)}, u32[]{:S(2)}, u32[]{:S(2)}) collective-permute-start(bf16[8,2,32,128]{3,2,1,0:T(8,128)(2,1)S(1)} %get-tuple-element.21), channel_id=1, source_target_pairs={{0,8},{8,16},{16,24},{24,0},{32,40},{40,48},{48,56},{56,32},{64,72... | collective-permute-start | bytes 393224 | tf_op jit(solution)/shard_map/ppermute | solution.py:238
  27.4 9.5 %collective-permute-start.3 = (bf16[8,2,32,128]{3,2,1,0:T(8,128)(2,1)S(1)}, bf16[8,2,32,128]{3,2,1,0:T(8,128)(2,1)S(1)}, u32[]{:S(2)}, u32[]{:S(2)}) collective-permute-start(bf16[8,2,32,128]{3,2,1,0:T(8,128)(2,1)S(1)} %get-tuple-element.20), channel_id=1, source_target_pairs={{0,24},{8,0},{16,8},{24,16},{32,56},{40,32},{48,40},{56,48},{64,88... | collective-permute-start | bytes 393224 | tf_op jit(solution)/shard_map/ppermute | solution.py:238
  30.0 7.0 %collective-permute-start.4 = (bf16[8,2,32,128]{3,2,1,0:T(8,128)(2,1)S(1)}, bf16[8,2,32,128]{3,2,1,0:T(8,128)(2,1)S(1)}, u32[]{:S(2)}, u32[]{:S(2)}) collective-permute-start(bf16[8,2,32,128]{3,2,1,0:T(8,128)(2,1)S(1)} %get-tuple-element.19), channel_id=1, source_target_pairs={{0,16},{8,24},{16,0},{24,8},{32,48},{40,56},{48,32},{56,40},{64,80... | collective-permute-start | bytes 393224 | tf_op jit(solution)/shard_map/ppermute | solution.py:238

commit v4 on v3

--- a/solution.py
+++ b/solution.py
@@ -87,7 +87,7 @@
         q = q_ref[:, h * HEAD : (h + 1) * HEAD]
         if not own:
             q = jnp.concatenate([q, one_s[...]], 1)
-        s_s[t % 2] = lax.dot_general(
+        s_s[t % 4] = lax.dot_general(
             k_s[g * per_item * rows : (g + 1) * per_item * rows],
             q,
             NT,
@@ -97,26 +97,26 @@
     def soften(t):
         _, g = items[t]
         for i in range(per_item):
-            x = s_s[t % 2, i * rows : (i + 1) * rows]
+            x = s_s[t % 4, i * rows : (i + 1) * rows]
             if own:
                 x = x + bias_s[...]
             top = jnp.max(x, 0, keepdims=True)
             expo = jnp.exp2((x - top) * EXP2_SCALE)
-            t_s[t % 2, i : i + 1] = top if own else top + query_bias
-            t_s[t % 2, 8 + i : 9 + i] = jnp.sum(expo, 0, keepdims=True)
-            p_s[t % 2, i * rows : (i + 1) * rows] = expo.astype(jnp.bfloat16)
+            t_s[t % 4, i : i + 1] = top if own else top + query_bias
+            t_s[t % 4, 8 + i : 9 + i] = jnp.sum(expo, 0, keepdims=True)
+            p_s[t % 4, i * rows : (i + 1) * rows] = expo.astype(jnp.bfloat16)
 
     def mix(t):
         h, g = items[t]
-        tops = [t_s[t % 2, i : i + 1] for i in range(per_item)]
-        totals = [t_s[t % 2, 8 + i : 9 + i] for i in range(per_item)]
+        tops = [t_s[t % 4, i : i + 1] for i in range(per_item)]
+        totals = [t_s[t % 4, 8 + i : 9 + i] for i in range(per_item)]
         best = functools.reduce(jnp.maximum, tops)
         acc = total = None
         if g > 0:
-            old = t_s[2 + h % 2, 0:1]
+            old = t_s[4 + h % 2, 0:1]
             best = jnp.maximum(best, old)
             f = jnp.exp2((old - best) * EXP2_SCALE)
-            acc, total = acc_s[h % 2] * f, t_s[2 + h % 2, 8:9] * f
+            acc, total = acc_s[h % 2] * f, t_s[4 + h % 2, 8:9] * f
         elif has_state:
             old = stat_in[h, 0:1]
             best = jnp.maximum(best, old)
@@ -126,7 +126,7 @@
             at = (g * per_item + i) * rows
             part = jnp.dot(
                 vt_s[:, at : at + rows],
-                p_s[t % 2, i * rows : (i + 1) * rows],
+                p_s[t % 4, i * rows : (i + 1) * rows],
                 preferred_element_type=jnp.float32,
             )
             f = jnp.exp2((tops[i] - best) * EXP2_SCALE)
@@ -134,8 +134,8 @@
             total = totals[i] * f if total is None else total + totals[i] * f
         if g < splits - 1:
             acc_s[h % 2] = acc
-            t_s[2 + h % 2, 0:1] = best
-            t_s[2 + h % 2, 8:9] = total
+            t_s[4 + h % 2, 0:1] = best
+            t_s[4 + h % 2, 8:9] = total
         elif final:
             out_s, sems = rest
             out_s[h] = (acc / total).astype(jnp.bfloat16).T
@@ -185,9 +185,9 @@
             pltpu.VMEM((HEAD, count * rows), jnp.bfloat16),
             pltpu.VMEM((rows, rows if own else HEAD), jnp.float32),
             pltpu.VMEM((rows, HEAD), jnp.bfloat16),
-            pltpu.VMEM((2, per_item * rows, rows), jnp.float32),
-            pltpu.VMEM((2, per_item * rows, rows), jnp.bfloat16),
-            pltpu.VMEM((4, 16, rows), jnp.float32),
+            pltpu.VMEM((4, per_item * rows, rows), jnp.float32),
+            pltpu.VMEM((4, per_item * rows, rows), jnp.bfloat16),
+            pltpu.VMEM((6, 16, rows), jnp.float32),
             pltpu.VMEM((2, HEAD, rows), jnp.float32),
         ]
         + (

time: 40.9 us -> 40.8 us (level)
  no operation moved by 1% of the time
where the time goes in v4:
time: 40.8 us; the launch traced here: 40.6 us
  starting transfers between devices  17.7 us (43%)
  blocking collectives  10.4 us (25%)
  Pallas kernels  10.1 us (25%)
  waiting for transfers between devices  1.28 us (3%)
  local copies, waits for them, and re-layouts  0.77 us (2%)
    ppermute x6, starting transfers between devices, around(): lax.ppermute(block, 'ctx', [(i, i - i % WIDE + (i + shift) % WIDE) for i...  10.9 us
    all_to_all x1, blocking collectives, on_device(): lax.all_to_all(pack(keys, values), 'kvg', split_axis=0, concat_axis=0, ti...  10.4 us
    pallas_call x3, Pallas kernels, attend(): pl.pallas_call(functools.partial(attend_kernel, plan, per_item, own, bool...  8.52 us
    ppermute x2, starting transfers between devices, back(): lax.ppermute(block, 'ctx', [(i, (i + distance) % blocks) for i in range(b...  6.82 us
    pallas_call x1, Pallas kernels, pack(): pl.pallas_call(functools.partial(pack_kernel, groups), in_specs=[VMEM, VM...  1.61 us
  transfers between devices with their start and end apart: 8, of which 2 were waited for; matrix products, arithmetic and copies ran while one was open for 0% of the time, Pallas kernels for 13%

profile of v4, /device:TPU:96, one launch (start us, length us, event | category | flops | bytes accessed | tf_op | source)
XLA Modules:
  0.0 40.6 jit_solution(436199296552345456)
XLA Ops:
  0.0 0.0 copy-start
  0.0 1.6 %shard_map.46 = bf16[8,2,32,128]{3,2,1,0:T(8,128)(2,1)} custom-call(bf16[32,1024]{1,0:T(8,128)(2,1)} %k_ref.1, bf16[32,1024]{1,0:T(8,128)(2,1)} %v_ref.1), custom_call_target="tpu_custom_call" | custom-call | tf_op jit(solution)/shard_map/pallas_call | solution.py:29
  1.6 10.4 %all_to_all.5.refs_3_ = bf16[8,2,32,128]{3,2,1,0:T(8,128)(2,1)S(1)} all-to-all(bf16[8,2,32,128]{3,2,1,0:T(8,128)(2,1)} %shard_map.46), channel_id=1, replica_groups=mesh['ctx'=32,'kvg'=8] {'kvg'}, dimensions={0} | all-to-all | bytes 262144 | tf_op jit(solution)/shard_map/all_to_all | solution.py:232
  12.0 3.1 %collective-permute-start = (bf16[8,2,32,128]{3,2,1,0:T(8,128)(2,1)S(1)}, bf16[8,2,32,128]{3,2,1,0:T(8,128)(2,1)S(1)}, u32[]{:S(2)}, u32[]{:S(2)}) collective-permute-start(bf16[8,2,32,128]{3,2,1,0:T(8,128)(2,1)S(1)} %all_to_all.5.refs_3_), channel_id=1, source_target_pairs={{0,32},{8,40},{16,48},{24,56},{32,64},{40,72},{48,80},{56,88},{64,... | collective-permute-start | bytes 393224 | tf_op jit(solution)/shard_map/ppermute | solution.py:235
  15.2 0.0 copy-done
  15.2 0.0 copy-start.1
  15.2 0.8 %copy-done.1 = s32[8192]{0:T(1024)S(1)} copy-done((s32[8192]{0:T(1024)S(1)}, s32[8192]{0:T(1024)}, u32[]{:S(2)}) %copy-start.1) | copy-done | bytes 32792
  15.9 1.3 %shard_map.47 = (f32[8,128,256]{2,1,0:T(8,128)S(1)}, f32[8,8,256]{2,1,0:T(8,128)S(1)}) custom-call(s32[1]{0:T(128)} %bitcast.refs_0_, bf16[256,1024]{1,0:T(8,128)(2,1)S(1)} %copy-done, s32[64,128]{1,0:T(8,128)S(1)} %bitcast.2, bf16[8,2,32,128]{3,2,1,0:T(8,128)(2,1)S(1)} %all_to_all.5.refs_3_), custom_call_target="tpu_custom_call" | custom-call | flops 268435456 | bytes 1048576 | tf_op jit(solution)/shard_map/pallas_call | solution.py:178
  17.2 0.5 %collective-permute-done.refs_3_ = bf16[8,2,32,128]{3,2,1,0:T(8,128)(2,1)S(1)} collective-permute-done((bf16[8,2,32,128]{3,2,1,0:T(8,128)(2,1)S(1)}, bf16[8,2,32,128]{3,2,1,0:T(8,128)(2,1)S(1)}, u32[]{:S(2)}, u32[]{:S(2)}) %collective-permute-start) | collective-permute-done | bytes 131104 | tf_op jit(solution)/shard_map/ppermute | solution.py:235
  17.7 3.7 %collective-permute-start.1 = (bf16[8,2,32,128]{3,2,1,0:T(8,128)(2,1)S(1)}, bf16[8,2,32,128]{3,2,1,0:T(8,128)(2,1)S(1)}, u32[]{:S(2)}, u32[]{:S(2)}) collective-permute-start(bf16[8,2,32,128]{3,2,1,0:T(8,128)(2,1)S(1)} %collective-permute-done.refs_3_), channel_id=1, source_target_pairs={{0,32},{8,40},{16,48},{24,56},{32,64},{40,72},{48,80},{56,88},{64,... | collective-permute-start | bytes 393224 | tf_op jit(solution)/shard_map/ppermute | solution.py:235
  21.4 0.0 copy-start.2
  21.4 1.6 %collective-permute-start.5 = (bf16[8,2,32,128]{3,2,1,0:T(8,128)(2,1)S(1)}, bf16[8,2,32,128]{3,2,1,0:T(8,128)(2,1)S(1)}, u32[]{:S(2)}, u32[]{:S(2)}) collective-permute-start(bf16[8,2,32,128]{3,2,1,0:T(8,128)(2,1)S(1)} %collective-permute-done.refs_3_), channel_id=1, source_target_pairs={{0,8},{8,16},{16,24},{24,0},{32,40},{40,48},{48,56},{56,32},{64,72... | collective-permute-start | bytes 393224 | tf_op jit(solution)/shard_map/ppermute | solution.py:238
  23.0 1.7 %collective-permute-start.6 = (bf16[8,2,32,128]{3,2,1,0:T(8,128)(2,1)S(1)}, bf16[8,2,32,128]{3,2,1,0:T(8,128)(2,1)S(1)}, u32[]{:S(2)}, u32[]{:S(2)}) collective-permute-start(bf16[8,2,32,128]{3,2,1,0:T(8,128)(2,1)S(1)} %collective-permute-done.refs_3_), channel_id=1, source_target_pairs={{0,24},{8,0},{16,8},{24,16},{32,56},{40,32},{48,40},{56,48},{64,88... | collective-permute-start | bytes 393224 | tf_op jit(solution)/shard_map/ppermute | solution.py:238
  24.7 2.0 %collective-permute-start.7 = (bf16[8,2,32,128]{3,2,1,0:T(8,128)(2,1)S(1)}, bf16[8,2,32,128]{3,2,1,0:T(8,128)(2,1)S(1)}, u32[]{:S(2)}, u32[]{:S(2)}) collective-permute-start(bf16[8,2,32,128]{3,2,1,0:T(8,128)(2,1)S(1)} %collective-permute-done.refs_3_), channel_id=1, source_target_pairs={{0,16},{8,24},{16,0},{24,8},{32,48},{40,56},{48,32},{56,40},{64,80... | collective-permute-start | bytes 393224 | tf_op jit(solution)/shard_map/ppermute | solution.py:238
  26.7 0.0 collective-permute-done.1.refs_4_
  26.7 0.8 %collective-permute-start.2 = (bf16[8,2,32,128]{3,2,1,0:T(8,128)(2,1)S(1)}, bf16[8,2,32,128]{3,2,1,0:T(8,128)(2,1)S(1)}, u32[]{:S(2)}, u32[]{:S(2)}) collective-permute-start(bf16[8,2,32,128]{3,2,1,0:T(8,128)(2,1)S(1)} %get-tuple-element.21), channel_id=1, source_target_pairs={{0,8},{8,16},{16,24},{24,0},{32,40},{40,48},{48,56},{56,32},{64,72... | collective-permute-start | bytes 393224 | tf_op jit(solution)/shard_map/ppermute | solution.py:238
  27.4 2.6 %collective-permute-start.3 = (bf16[8,2,32,128]{3,2,1,0:T(8,128)(2,1)S(1)}, bf16[8,2,32,128]{3,2,1,0:T(8,128)(2,1)S(1)}, u32[]{:S(2)}, u32[]{:S(2)}) collective-permute-start(bf16[8,2,32,128]{3,2,1,0:T(8,128)(2,1)S(1)} %get-tuple-element.20), channel_id=1, source_target_pairs={{0,24},{8,0},{16,8},{24,16},{32,56},{40,32},{48,40},{56,48},{64,88... | collective-permute-start | bytes 393224 | tf_op jit(solution)/shard_map/ppermute | solution.py:238
  30.0 0.0 collective-permute-done.5.refs_5_
  30.0 2.4 %collective-permute-start.4 = (bf16[8,2,32,128]{3,2,1,0:T(8,128)(2,1)S(1)}, bf16[8,2,32,128]{3,2,1,0:T(8,128)(2,1)S(1)}, u32[]{:S(2)}, u32[]{:S(2)}) collective-permute-start(bf16[8,2,32,128]{3,2,1,0:T(8,128)(2,1)S(1)} %get-tuple-element.19), channel_id=1, source_target_pairs={{0,16},{8,24},{16,0},{24,8},{32,48},{40,56},{48,32},{56,40},{64,80... | collective-permute-start | bytes 393224 | tf_op jit(solution)/shard_map/ppermute | solution.py:238
  32.4 0.0 collective-permute-done.6.refs_6_
  32.4 0.7 %collective-permute-done.7.refs_7_ = bf16[8,2,32,128]{3,2,1,0:T(8,128)(2,1)S(1)} collective-permute-done((bf16[8,2,32,128]{3,2,1,0:T(8,128)(2,1)S(1)}, bf16[8,2,32,128]{3,2,1,0:T(8,128)(2,1)S(1)}, u32[]{:S(2)}, u32[]{:S(2)}) %collective-permute-start.7) | collective-permute-done | bytes 131104 | tf_op jit(solution)/shard_map/ppermute | solution.py:238
  33.1 0.0 copy-done.2
  33.1 3.8 %shard_map.48 = (f32[8,128,256]{2,1,0:T(8,128)S(1)}, f32[8,8,256]{2,1,0:T(8,128)S(1)}) custom-call(s32[1]{0:T(128)} %bitcast.refs_0_, bf16[256,1024]{1,0:T(8,128)(2,1)S(1)} %copy-done, s32[64,128]{1,0:T(8,128)S(1)} %bitcast.3, bf16[8,2,32,128]{3,2,1,0:T(8,128)(2,1)S(1)} %collective-permute-done.refs_3_, ...), custom_call_target="tpu_custom_call" | custom-call | flops 1342177280 | bytes 1048576 | tf_op jit(solution)/shard_map/pallas_call | solution.py:178
  37.0 0.0 collective-permute-done.2.refs_3_
  37.0 0.0 collective-permute-done.3.refs_4_
  37.0 0.0 collective-permute-done.4.refs_5_
  37.0 3.4 %shard_map.49 = bf16[256,1024]{1,0:T(8,128)(2,1)} custom-call(s32[1]{0:T(128)} %bitcast.refs_0_, bf16[256,1024]{1,0:T(8,128)(2,1)S(1)} %copy-done, s32[64,128]{1,0:T(8,128)S(1)} %bitcast.4, bf16[8,2,32,128]{3,2,1,0:T(8,128)(2,1)S(1)} %collective-permute-done.2.refs_3_, bf16[8,2,32,128]{3,2,1,0:T(8,128)(2,1)S(1)} %collective-permute-done.3.refs_4_, ...), custom_call_target="tpu_custom_call" | custom-call | flops 805306368 | bytes 1048576 | tf_op jit(solution)/shard_map/pallas_call | solution.py:178
  (1 shorter events, 0.0 us)
Async XLA Ops:
  0.0 15.2 %copy-start = (bf16[256,1024]{1,0:T(8,128)(2,1)S(1)}, bf16[256,1024]{1,0:T(8,128)(2,1)}, u32[]{:S(2)}) copy-start(bf16[256,1024]{1,0:T(8,128)(2,1)} %refs_1_.5) | copy-start | bytes 1572868
  12.0 5.7 %collective-permute-start = (bf16[8,2,32,128]{3,2,1,0:T(8,128)(2,1)S(1)}, bf16[8,2,32,128]{3,2,1,0:T(8,128)(2,1)S(1)}, u32[]{:S(2)}, u32[]{:S(2)}) collective-permute-start(bf16[8,2,32,128]{3,2,1,0:T(8,128)(2,1)S(1)} %all_to_all.5.refs_3_), channel_id=1, source_target_pairs={{0,32},{8,40},{16,48},{24,56},{32,64},{40,72},{48,80},{56,88},{64,... | collective-permute-start | bytes 393224 | tf_op jit(solution)/shard_map/ppermute | solution.py:235
  15.2 0.8 %copy-start.1 = (s32[8192]{0:T(1024)S(1)}, s32[8192]{0:T(1024)}, u32[]{:S(2)}) copy-start(s32[8192]{0:T(1024)} %param.7) | copy-start | bytes 98308
  17.7 8.9 %collective-permute-start.1 = (bf16[8,2,32,128]{3,2,1,0:T(8,128)(2,1)S(1)}, bf16[8,2,32,128]{3,2,1,0:T(8,128)(2,1)S(1)}, u32[]{:S(2)}, u32[]{:S(2)}) collective-permute-start(bf16[8,2,32,128]{3,2,1,0:T(8,128)(2,1)S(1)} %collective-permute-done.refs_3_), channel_id=1, source_target_pairs={{0,32},{8,40},{16,48},{24,56},{32,64},{40,72},{48,80},{56,88},{64,... | collective-permute-start | bytes 393224 | tf_op jit(solution)/shard_map/ppermute | solution.py:235
  21.4 11.7 %copy-start.2 = (s32[8192]{0:T(1024)S(1)}, s32[8192]{0:T(1024)}, u32[]{:S(2)}) copy-start(s32[8192]{0:T(1024)} %param.7) | copy-start | bytes 98308
  21.4 8.6 %collective-permute-start.5 = (bf16[8,2,32,128]{3,2,1,0:T(8,128)(2,1)S(1)}, bf16[8,2,32,128]{3,2,1,0:T(8,128)(2,1)S(1)}, u32[]{:S(2)}, u32[]{:S(2)}) collective-permute-start(bf16[8,2,32,128]{3,2,1,0:T(8,128)(2,1)S(1)} %collective-permute-done.refs_3_), channel_id=1, source_target_pairs={{0,8},{8,16},{16,24},{24,0},{32,40},{40,48},{48,56},{56,32},{64,72... | collective-permute-start | bytes 393224 | tf_op jit(solution)/shard_map/ppermute | solution.py:238
  23.0 9.4 %collective-permute-start.6 = (bf16[8,2,32,128]{3,2,1,0:T(8,128)(2,1)S(1)}, bf16[8,2,32,128]{3,2,1,0:T(8,128)(2,1)S(1)}, u32[]{:S(2)}, u32[]{:S(2)}) collective-permute-start(bf16[8,2,32,128]{3,2,1,0:T(8,128)(2,1)S(1)} %collective-permute-done.refs_3_), channel_id=1, source_target_pairs={{0,24},{8,0},{16,8},{24,16},{32,56},{40,32},{48,40},{56,48},{64,88... | collective-permute-start | bytes 393224 | tf_op jit(solution)/shard_map/ppermute | solution.py:238
  24.7 8.5 %collective-permute-start.7 = (bf16[8,2,32,128]{3,2,1,0:T(8,128)(2,1)S(1)}, bf16[8,2,32,128]{3,2,1,0:T(8,128)(2,1)S(1)}, u32[]{:S(2)}, u32[]{:S(2)}) collective-permute-start(bf16[8,2,32,128]{3,2,1,0:T(8,128)(2,1)S(1)} %collective-permute-done.refs_3_), channel_id=1, source_target_pairs={{0,16},{8,24},{16,0},{24,8},{32,48},{40,56},{48,32},{56,40},{64,80... | collective-permute-start | bytes 393224 | tf_op jit(solution)/shard_map/ppermute | solution.py:238
  26.7 10.3 %collective-permute-start.2 = (bf16[8,2,32,128]{3,2,1,0:T(8,128)(2,1)S(1)}, bf16[8,2,32,128]{3,2,1,0:T(8,128)(2,1)S(1)}, u32[]{:S(2)}, u32[]{:S(2)}) collective-permute-start(bf16[8,2,32,128]{3,2,1,0:T(8,128)(2,1)S(1)} %get-tuple-element.21), channel_id=1, source_target_pairs={{0,8},{8,16},{16,24},{24,0},{32,40},{40,48},{48,56},{56,32},{64,72... | collective-permute-start | bytes 393224 | tf_op jit(solution)/shard_map/ppermute | solution.py:238
  27.4 9.5 %collective-permute-start.3 = (bf16[8,2,32,128]{3,2,1,0:T(8,128)(2,1)S(1)}, bf16[8,2,32,128]{3,2,1,0:T(8,128)(2,1)S(1)}, u32[]{:S(2)}, u32[]{:S(2)}) collective-permute-start(bf16[8,2,32,128]{3,2,1,0:T(8,128)(2,1)S(1)} %get-tuple-element.20), channel_id=1, source_target_pairs={{0,24},{8,0},{16,8},{24,16},{32,56},{40,32},{48,40},{56,48},{64,88... | collective-permute-start | bytes 393224 | tf_op jit(solution)/shard_map/ppermute | solution.py:238
  30.0 7.0 %collective-permute-start.4 = (bf16[8,2,32,128]{3,2,1,0:T(8,128)(2,1)S(1)}, bf16[8,2,32,128]{3,2,1,0:T(8,128)(2,1)S(1)}, u32[]{:S(2)}, u32[]{:S(2)}) collective-permute-start(bf16[8,2,32,128]{3,2,1,0:T(8,128)(2,1)S(1)} %get-tuple-element.19), channel_id=1, source_target_pairs={{0,16},{8,24},{16,0},{24,8},{32,48},{40,56},{48,32},{56,40},{64,80... | collective-permute-start | bytes 393224 | tf_op jit(solution)/shard_map/ppermute | solution.py:238
